TPU v7x, 32 devices: a whole 2x2x4 slice. The times are simulated.
32 devices in a mesh: head: 4 (over y, x), blk: 4 (over z), dp: 2 (over core).
Axes of the slice: x: 2, y: 2, z: 4, core: 2. Of those that a mesh axis runs over, the one named last changes fastest.
Arguments:
- layer_input: bfloat16 [4096, 4096], P(('dp', 'blk', 'head')), may hold values from -6 to 6
- rot_queries: bfloat16 [4096, 4096], P(('dp', 'blk', 'head')), may hold values from -6 to 6
- rot_keys: bfloat16 [4096, 512], P(('dp', 'blk', 'head')), may hold values from -6 to 6
- value_rows: bfloat16 [4096, 512], P(('dp', 'blk', 'head')), may hold values from -6 to 6
- attn_output: bfloat16 [4096, 4096], P(('dp', 'blk', 'head')), may hold values from -3 to 3
- output_grad: bfloat16 [4096, 4096], P(('dp', 'blk', 'head')), may hold values from -1.5 to 1.5
- log_norm: float32 [4096, 32], P(('dp', 'blk'), 'head'), may hold values from 6 to 8
- lengths: int32 [2, 3], P('dp'), may hold values from 128 to 1280, as said below
Outputs:
- dw_query: float32 [4096, 4096], P(('blk', 'dp'), 'head')
- dw_key: float32 [4096, 512], P(('blk', 'dp'), 'head')
- dw_value: float32 [4096, 512], P(('blk', 'dp'), 'head')
Inputs may be any that keep to these rules, and one draw needn't show every extreme that they name: `lengths`: each row sums to 2048; every length is a multiple of 128; in every row one document has length 1280.
All inputs are finite; a program needn't handle non-finite values.
Results may differ from a plain program's by a relative error of at most 0.0041.
Values may be sent and summed in bfloat16 or wider, within the bound.
A program may use at most 128 MiB of HBM per device.

v0:
```python
import math

import jax
import jax.numpy as jnp
from jax import lax
from jax.sharding import PartitionSpec as P

HQ = 32
HD = 128
GQ = 8


def contract_rows(left, right):
    return lax.dot_general(
        left, right, (((0,), (0,)), ((), ())), preferred_element_type=jnp.float32
    )


def contract_cols(left, right):
    return lax.dot_general(
        left, right, (((1,), (1,)), ((), ())), preferred_element_type=jnp.float32
    )


def doc_place(ends, lengths_row, index):
    after = (index[:, None] >= ends[None, :]).astype(jnp.int32)
    doc = jnp.sum(after, axis=1)
    first = jnp.sum(after * lengths_row[None, :], axis=1)
    return (doc, index - first)


def undo_rotary(grad, position):
    half = grad.shape[2] // 2
    steps_j = jnp.arange(half).astype(jnp.float32)
    inverse = jnp.exp(-math.log(500000.0) * 2.0 * steps_j / grad.shape[2])
    angle = position.astype(jnp.float32)[:, None] * inverse[None, :]
    cosine = jnp.cos(angle)[:, None, :]
    sine = jnp.sin(angle)[:, None, :]
    first = grad[:, :, :half]
    second = grad[:, :, half:]
    return jnp.concatenate([first * cosine + second * sine, second * cosine - first * sine], axis=2)


def on_device(
    layer_input, rot_queries, rot_keys, value_rows, attn_output, output_grad, log_norm, lengths
):
    head_count = log_norm.shape[1]
    kv_count = head_count // GQ
    scale = HD ** (-0.5)
    local_count = rot_queries.shape[0]
    own_delta = jnp.sum(
        (output_grad.astype(jnp.float32) * attn_output.astype(jnp.float32)).reshape(
            local_count, HQ, HD
        ),
        axis=2,
    )
    queries, grads_out, keys_here, values_here = (
        lax.all_to_all(rot_queries, "head", split_axis=1, concat_axis=0, tiled=True),
        lax.all_to_all(output_grad, "head", split_axis=1, concat_axis=0, tiled=True),
        lax.all_to_all(rot_keys, "head", split_axis=1, concat_axis=0, tiled=True),
        lax.all_to_all(value_rows, "head", split_axis=1, concat_axis=0, tiled=True),
    )
    delta = lax.all_to_all(own_delta, "head", split_axis=1, concat_axis=0, tiled=True)
    row_count = queries.shape[0]
    inputs_here = lax.all_gather(layer_input, "head", axis=0, tiled=True)
    cycle_count = lax.axis_size("blk")
    lengths_row = lengths[0]
    ends = jnp.cumsum(lengths_row)
    first_row = lax.axis_index("blk") * row_count
    last_row = first_row + row_count - 1
    query_index = first_row + jnp.arange(row_count, dtype=jnp.int32)
    query_doc, query_pos = doc_place(ends, lengths_row, query_index)
    initial = (
        jnp.zeros((row_count, head_count * HD), jnp.float32),
        jnp.zeros((row_count * cycle_count, kv_count * HD), jnp.float32),
        jnp.zeros((row_count * cycle_count, kv_count * HD), jnp.float32),
    )
    start = jnp.int32(0)
    key_piece = lax.all_gather(keys_here, "blk", axis=0, tiled=True)
    value_piece = lax.all_gather(values_here, "blk", axis=0, tiled=True)
    key_count = key_piece.shape[0]

    def compute(state):
        dq_all, dk_all, dv_all = state
        key_index = jnp.arange(key_count, dtype=jnp.int32)
        key_doc, _ = doc_place(ends, lengths_row, key_index)
        allowed = (query_doc[:, None] == key_doc[None, :]) & (
            key_index[None, :] <= query_index[:, None]
        )
        dq_parts = []
        dk_block = jnp.zeros((key_count, HD), jnp.float32)
        dv_block = jnp.zeros((key_count, HD), jnp.float32)
        for member in range(GQ):
            query_block = queries[:, member * HD : (member + 1) * HD]
            grad_block = grads_out[:, member * HD : (member + 1) * HD]
            score = contract_cols(query_block, key_piece) * scale
            prob = jnp.where(allowed, jnp.exp(score - log_norm[:, member : member + 1]), 0.0)
            dprob = contract_cols(grad_block, value_piece)
            dscore = prob * (dprob - delta[:, member : member + 1])
            prob_low = prob.astype(jnp.bfloat16)
            dscore_low = dscore.astype(jnp.bfloat16)
            dq_parts.append(
                jnp.dot(dscore_low, key_piece, preferred_element_type=jnp.float32) * scale
            )
            dk_block = dk_block + contract_rows(dscore_low, query_block) * scale
            dv_block = dv_block + contract_rows(prob_low, grad_block)
        dk_parts = [dk_block]
        dv_parts = [dv_block]
        dq_all = dq_all + jnp.concatenate(dq_parts, axis=1)
        old_keys = dk_all
        dk_all = lax.dynamic_update_slice_in_dim(
            dk_all, old_keys + jnp.concatenate(dk_parts, axis=1), start, 0
        )
        old_values = dv_all
        dv_all = lax.dynamic_update_slice_in_dim(
            dv_all, old_values + jnp.concatenate(dv_parts, axis=1), start, 0
        )
        return (dq_all, dk_all, dv_all)

    nearest = jnp.minimum(start + key_count - 1, last_row)
    near_doc = jnp.sum((nearest >= ends).astype(jnp.int32))
    visible = (start <= last_row) & (near_doc >= query_doc[0])
    result = lax.cond(visible, compute, lambda state: state, initial)
    dq_sum, dk_part, dv_part = result
    dk_sum, dv_sum = (
        lax.psum_scatter(dk_part, "blk", scatter_dimension=0, tiled=True),
        lax.psum_scatter(dv_part, "blk", scatter_dimension=0, tiled=True),
    )
    dq_low = (
        undo_rotary(dq_sum.reshape(row_count, head_count, HD), query_pos)
        .reshape(row_count, head_count * HD)
        .astype(jnp.bfloat16)
    )
    dk_low = (
        undo_rotary(dk_sum.reshape(row_count, kv_count, HD), query_pos)
        .reshape(row_count, kv_count * HD)
        .astype(jnp.bfloat16)
    )
    dv_low = dv_sum.astype(jnp.bfloat16)
    token_grads = jnp.concatenate([dq_low, dk_low, dv_low], axis=1)
    summed = lax.psum_scatter(
        contract_rows(inputs_here, token_grads), ("blk", "dp"), scatter_dimension=0, tiled=True
    )
    query_width = head_count * HD
    key_width = kv_count * HD
    return (
        summed[:, :query_width],
        summed[:, query_width : query_width + key_width],
        summed[:, query_width + key_width :],
    )


def solution(mesh):
    placed = (
        P(("dp", "blk", "head"), None),
        P(("dp", "blk", "head"), None),
        P(("dp", "blk", "head"), None),
        P(("dp", "blk", "head"), None),
        P(("dp", "blk", "head"), None),
        P(("dp", "blk", "head"), None),
        P(("dp", "blk"), "head"),
        P("dp", None),
    )
    return jax.shard_map(
        on_device,
        mesh=mesh,
        in_specs=placed,
        out_specs=(P(("blk", "dp"), "head"), P(("blk", "dp"), "head"), P(("blk", "dp"), "head")),
        check_vma=False,
    )
```

profile of v0, /device:TPU:0, one launch (start us, length us, event | category | flops | bytes accessed | tf_op | source)
XLA Modules:
  0.0 434.7 jit_solution(1058754098441431327)
XLA Ops:
  8.0 1.8 multiply_bitcast_fusion
  11.5 5.2 %all-to-all-start.4 = ((f32[128,4,8]{0,2,1:T(8,128)}), f32[128,4,8]{0,2,1:T(8,128)S(1)}, u32[]{:S(2)}, u32[]{:S(2)}) async-start(f32[128,4,8]{0,2,1:T(8,128)} %bitcast.31), calls=%async_computation.4 | async-start | bytes 32768 | tf_op jit(solution)/shard_map/all_to_all | solution.py:63
  17.4 4.0 all-to-all-done.4
  21.4 3.3 all-to-all-start.1
  25.4 4.3 all-to-all-done.1
  29.7 3.3 all-to-all-start.3
  33.1 2.3 copy.66
  35.4 2.7 all-to-all-done.3
  38.1 3.5 all-to-all-start
  41.6 2.3 copy.68
  43.9 7.9 %all-to-all-done = bf16[128,4,1024]{0,2,1:T(8,128)(2,1)S(1)} async-done(((bf16[128,4,1024]{0,2,1:T(8,128)(2,1)}), bf16[128,4,1024]{0,2,1:T(8,128)(2,1)S(1)}, u32[]{:S(2)}, u32[]{:S(2)}) %all-to-all-start) | async-done | bytes 1048608 | tf_op jit(solution)/shard_map/all_to_all | solution.py:58
  51.8 3.5 all-to-all-start.2
  58.1 16.8 %all_gather.10 = bf16[2048,128]{1,0:T(8,128)(2,1)S(1)} all-gather(bf16[512,128]{1,0:T(8,128)(2,1)S(1)} %bitcast.135), channel_id=1, replica_groups=mesh['head'=4,'blk'=4,'dp'=2] {'blk'}, dimensions={0}, use_global_device_ids=true | all-gather | bytes 655360 | tf_op jit(solution)/shard_map/all_gather | solution.py:80
  74.9 14.9 %all_gather.9 = bf16[2048,128]{1,0:T(8,128)(2,1)S(1)} all-gather(bf16[512,128]{1,0:T(8,128)(2,1)S(1)} %bitcast.134), channel_id=1, replica_groups=mesh['head'=4,'blk'=4,'dp'=2] {'blk'}, dimensions={0}, use_global_device_ids=true | all-gather | bytes 655360 | tf_op jit(solution)/shard_map/all_gather | solution.py:79
  89.8 51.3 %conditional.1 = (f32[2048,128]{1,0:T(8,128)}, f32[2048,128]{1,0:T(8,128)}, f32[512,8,64]{0,2,1:T(8,128)}, f32[512,8,64]{0,2,1:T(8,128)S(1)}) conditional(s32[]{:T(128)} %convert_element_type.114, () %tuple.22, (s32[512]{0:T(512)S(1)}, s32[3]{0:T(128)S(1)}, s32[]{:T(128)}, s32[512]{0:T(512)S(1)}, bf16[4,128,1024]{1,2,0:T(8,128)(2,1)S(1)}, ...), branch_computations={%region_4.5_spmd, %region_5.7_spmd} | conditional | flops 10825777152 | bytes 298004704 | solution.py:123
  109.1 2.0 copy-done.5
  116.3 3.1 convolution_add_fusion.5
  122.9 1.8 convolution_add_fusion
  141.2 2.5 copy.73
  146.6 23.6 %reduce-scatter.6.cloned.1.call-done = f32[512,128]{1,0:T(8,128)} async-done(((f32[2048,128]{1,0:T(8,128)}), f32[512,128]{1,0:T(8,128)}) %reduce-scatter.6.cloned.1.call-update) | async-done | bytes 262160 | tf_op jit(solution)/shard_map/reduce_scatter | solution.py:127
  171.3 27.1 %reduce-scatter.4.cloned.1.call-done = f32[512,128]{0,1:T(8,128)} async-done(((f32[2048,128]{0,1:T(8,128)}), f32[512,128]{0,1:T(8,128)}) %reduce-scatter.4.cloned.1.call-update) | async-done | bytes 262160 | tf_op jit(solution)/shard_map/reduce_scatter | solution.py:126
  200.4 13.0 %convolution_bitcast_fusion = f32[4096,1280]{0,1:T(8,128)} fusion(bf16[512,4096]{1,0:T(8,128)(2,1)} %all-gather.2.cloned.1.call-done, bf16[512,128]{0,1:T(8,128)(2,1)S(1)} %copy.74, bf16[512,128]{0,1:T(8,128)(2,1)S(1)} %maximum_bitcast_fusion, bf16[512,1024]{0,1:T(8,128)(2,1)S(1)} %bitcast.133), kind=kOutput, calls=%fused_computation.94 | convolution fusion | flops 5372641280 | bytes 26476544 | tf_op jit(solution)/shard_map/dot_general | solution.py:14
  213.4 207.9 %reduce-scatter.8.cloned.1.call-done = f32[512,1280]{0,1:T(8,128)} async-done(((f32[4096,1280]{0,1:T(8,128)}), f32[512,1280]{0,1:T(8,128)}) %reduce-scatter.8.cloned.1.call-update) | async-done | bytes 2621456 | tf_op jit(solution)/shard_map/reduce_scatter | solution.py:141
  422.8 1.8 copy.75
  (101 shorter events, 58.7 us)
Async XLA Ops:
  8.0 8.7 %copy-start = (bf16[128,512]{1,0:T(8,128)(2,1)S(1)}, bf16[128,512]{1,0:T(8,128)(2,1)}, u32[]{:S(2)}) copy-start(bf16[128,512]{1,0:T(8,128)(2,1)} %param.12) | copy-start | bytes 393220
  9.9 14.9 %copy-start.8 = (bf16[128,512]{1,0:T(8,128)(2,1)S(1)}, bf16[128,512]{1,0:T(8,128)(2,1)}, u32[]{:S(2)}) copy-start(bf16[128,512]{1,0:T(8,128)(2,1)} %param.13) | copy-start | bytes 393220
  11.5 9.9 %all-to-all-start.4 = ((f32[128,4,8]{0,2,1:T(8,128)}), f32[128,4,8]{0,2,1:T(8,128)S(1)}, u32[]{:S(2)}, u32[]{:S(2)}) async-start(f32[128,4,8]{0,2,1:T(8,128)} %bitcast.31), calls=%async_computation.4 | async-start | bytes 32768 | tf_op jit(solution)/shard_map/all_to_all | solution.py:63
  21.4 8.3 %all-to-all-start.1 = ((bf16[128,4,128]{2,0,1:T(8,128)(2,1)}), bf16[128,4,128]{2,0,1:T(8,128)(2,1)S(1)}, u32[]{:S(2)}, u32[]{:S(2)}) async-start(bf16[128,4,128]{2,0,1:T(8,128)(2,1)} %copy_bitcast_fusion.1), calls=%async_computation.1 | async-start | bytes 262144 | tf_op jit(solution)/shard_map/all_to_all | solution.py:60
  29.7 8.3 %all-to-all-start.3 = ((bf16[128,4,128]{2,0,1:T(8,128)(2,1)}), bf16[128,4,128]{2,0,1:T(8,128)(2,1)S(1)}, u32[]{:S(2)}, u32[]{:S(2)}) async-start(bf16[128,4,128]{2,0,1:T(8,128)(2,1)} %copy_bitcast_fusion), calls=%async_computation.3 | async-start | bytes 262144 | tf_op jit(solution)/shard_map/all_to_all | solution.py:61
  33.1 22.3 %copy-start.10 = (s32[1,3]{1,0:T(1,128)S(1)}, s32[1,3]{1,0:T(1,128)}, u32[]{:S(2)}) copy-start(s32[1,3]{1,0:T(1,128)} %param.17) | copy-start | bytes 40
  35.3 54.4 %copy-start.9 = (f32[512,8]{0,1:T(8,128)S(1)}, f32[512,8]{0,1:T(8,128)}, u32[]{:S(2)}) copy-start(f32[512,8]{0,1:T(8,128)} %param.16) | copy-start | bytes 49156
  38.1 13.7 %all-to-all-start = ((bf16[128,4,1024]{0,2,1:T(8,128)(2,1)}), bf16[128,4,1024]{0,2,1:T(8,128)(2,1)S(1)}, u32[]{:S(2)}, u32[]{:S(2)}) async-start(bf16[128,4,1024]{0,2,1:T(8,128)(2,1)} %bitcast.23), calls=%async_computation | async-start | bytes 2097152 | tf_op jit(solution)/shard_map/all_to_all | solution.py:58
  51.8 38.0 %all-to-all-start.2 = ((bf16[128,4,1024]{0,2,1:T(8,128)(2,1)}), bf16[128,4,1024]{0,2,1:T(8,128)(2,1)S(1)}, u32[]{:S(2)}, u32[]{:S(2)}) async-start(bf16[128,4,1024]{0,2,1:T(8,128)(2,1)} %bitcast.27), calls=%async_computation.2 | async-start | bytes 2097152 | tf_op jit(solution)/shard_map/all_to_all | solution.py:59
  55.3 114.9 %reduce-scatter.6.cloned.1.call-start = ((), (), s32[]{:S(2)}) async-start(), calls=%async_computation.9 | async-start | bytes 1310720 | tf_op jit(solution)/shard_map/reduce_scatter | solution.py:127
  89.8 1.0 copy-start.7
  103.3 2.0 copy-start.2
  106.7 2.4 copy-start.4
  109.1 2.0 copy-start.5
  113.3 2.2 copy-start.6
  116.3 3.5 copy-start.3
  141.2 57.3 %reduce-scatter.4.cloned.1.call-start = ((), (), s32[]{:S(2)}) async-start(), calls=%async_computation.8 | async-start | bytes 1310720 | tf_op jit(solution)/shard_map/reduce_scatter | solution.py:126
  143.8 56.6 %all-gather.2.cloned.1.call-start = ((), (), s32[]{:S(2)}) async-start(), calls=%async_computation.10 | async-start | bytes 5242880 | tf_op jit(solution)/shard_map/all_gather | solution.py:65
  144.4 276.9 %reduce-scatter.8.cloned.1.call-start = ((), (), s32[]{:S(2)}) async-start(), calls=%async_computation.11 | async-start | bytes 23592960 | tf_op jit(solution)/shard_map/reduce_scatter | solution.py:141
  421.2 1.6 slice-start
  421.2 6.1 %copy-start.1 = (bf16[128,512]{1,0:T(8,128)(2,1)S(1)}, bf16[128,512]{1,0:T(8,128)(2,1)}, u32[]{:S(2)}) copy-start(bf16[128,512]{1,0:T(8,128)(2,1)} %param.12) | copy-start | bytes 393220
Sparse Core Ops, SparseCore 0:
  141.3 28.8 reduce-scatter.5
  172.6 25.7 reduce-scatter.3
  213.5 207.6 reduce-scatter.7
Sparse Core Ops, SparseCore 1:
  146.1 54.2 all-gather.1
where the time goes:
time: 439 us; the launch traced here: 435 us
  waiting for transfers between devices  279 us (64%)
  matrix products  54.6 us (12%)
  blocking collectives  31.7 us (7%)
  local copies, waits for them, and re-layouts  25.4 us (6%)
  starting transfers between devices  19 us (4%)
  between operations  16.9 us (4%)
  other arithmetic  8.12 us (2%)
    reduce_scatter x1, waiting for transfers between devices, on_device(): lax.psum_scatter(contract_rows(inputs_here, token_grads), ('blk', 'dp'),...  208 us
    dot_general x17, matrix products, contract_rows(): lax.dot_general(left, right, (((0,), (0,)), ((), ())), preferred_element_...  29.8 us
    reduce_scatter x1, waiting for transfers between devices, on_device(): lax.psum_scatter(dk_part, 'blk', scatter_dimension=0, tiled=True)  27.1 us
    reduce_scatter x1, waiting for transfers between devices, on_device(): lax.psum_scatter(dv_part, 'blk', scatter_dimension=0, tiled=True)  23.6 us
    dot_general x16, matrix products, contract_cols(): lax.dot_general(left, right, (((1,), (1,)), ((), ())), preferred_element_...  17.7 us
    all_gather x1, blocking collectives, on_device(): value_piece = lax.all_gather(values_here, 'blk', axis=0, tiled=True)  16.8 us
    all_gather x1, blocking collectives, on_device(): key_piece = lax.all_gather(keys_here, 'blk', axis=0, tiled=True)  14.9 us
  transfers between devices with their start and end apart: 9, of which 8 were waited for; matrix products, arithmetic and copies ran while one was open for 3% of the time, Pallas kernels for 0%

commit v1 on v0

v1 whole, which is shorter than its diff:
```python
import functools
import math

import jax
import jax.numpy as jnp
from jax import lax
from jax.experimental import pallas as pl
from jax.experimental.pallas import tpu as pltpu
from jax.sharding import PartitionSpec as P

HQ = 32
HD = 128
GQ = 8
UNIT = 128
MOST_LEN = 1280
BACK = MOST_LEN - UNIT
TILE = 256
LOG2E = math.log2(math.e)
SCALE = HD ** (-0.5)


def contract_rows(left, right):
    return lax.dot_general(
        left, right, (((0,), (0,)), ((), ())), preferred_element_type=jnp.float32
    )


def contract_cols(left, right):
    return lax.dot_general(
        left, right, (((1,), (1,)), ((), ())), preferred_element_type=jnp.float32
    )


def doc_place(ends, lengths_row, index):
    after = (index[:, None] >= ends[None, :]).astype(jnp.int32)
    first = jnp.sum(after * lengths_row[None, :], axis=1)
    return (first, index - first)


def attention_kernel(
    chunk, q_ref, g_ref, k_ref, v_ref, kt_ref, norm_ref, delta_ref, start_ref, cos_ref, sin_ref,
    dk_in_ref, dv_in_ref, dq_ref, dk_ref, dv_ref, bias_ref
):
    rows = q_ref.shape[0]
    tiles = rows // TILE
    span = TILE + BACK

    @pl.when(pl.program_id(0) == 0)
    def _():
        dk_ref[...] = dk_in_ref[...]
        dv_ref[...] = dv_in_ref[...]
        for j in range(tiles):
            key_at = lax.broadcasted_iota(jnp.int32, (span, TILE), 0) + j * TILE
            query_at = lax.broadcasted_iota(jnp.int32, (span, TILE), 1) + (j * TILE + BACK)
            first = start_ref[:, j * TILE : (j + 1) * TILE]
            allowed = (key_at >= first) & (key_at <= query_at)
            bias_ref[j] = jnp.where(allowed, 0.0, -1e30)

    for j in range(tiles):
        here = slice(j * TILE, (j + 1) * TILE)
        query = q_ref[here, :]
        grad = g_ref[here, :]
        norm = norm_ref[0, :, here]
        delta = delta_ref[0, :, here]
        dq_t = jnp.zeros((HD, TILE), jnp.float32)
        for c in range(0, span, chunk):
            keys = slice(j * TILE + c, j * TILE + c + chunk)
            score = contract_cols(k_ref[keys, :], query)
            prob = jnp.exp2((score * (SCALE * LOG2E) - norm) + bias_ref[j, c : c + chunk, :])
            dprob = contract_cols(v_ref[keys, :], grad)
            dscore = (prob * (dprob - delta)).astype(jnp.bfloat16)
            dv_ref[keys, :] += jnp.dot(
                prob.astype(jnp.bfloat16), grad, preferred_element_type=jnp.float32
            )
            dk_ref[keys, :] += jnp.dot(dscore, query, preferred_element_type=jnp.float32)
            dq_t += jnp.dot(kt_ref[:, keys], dscore, preferred_element_type=jnp.float32)
        cosine = cos_ref[:, here]
        sine = sin_ref[:, here]
        upper = dq_t[: HD // 2]
        lower = dq_t[HD // 2 :]
        turned = jnp.concatenate(
            [upper * cosine + lower * sine, lower * cosine - upper * sine], axis=0
        )
        dq_ref[here, :] = turned.T.astype(jnp.bfloat16)


def attention(first_head, heads, chunk, queries, grads, keys, values, keys_t, norm, delta, start,
              cosine, sine, dk_in, dv_in):
    rows = queries.shape[0]
    window = keys.shape[0]
    whole = lambda shape: pl.BlockSpec(shape, lambda h: (0,) * len(shape))
    per_head = pl.BlockSpec((rows, HD), lambda h: (0, h + first_head))
    per_row = pl.BlockSpec((1, 1, rows), lambda h: (h + first_head, 0, 0))
    work = heads * (rows // TILE) * (TILE + BACK) * TILE
    return pl.pallas_call(
        functools.partial(attention_kernel, chunk),
        grid=(heads,),
        in_specs=[
            per_head, per_head, whole((window, HD)), whole((window, HD)), whole((HD, window)),
            per_row, per_row, whole((1, rows)), whole((HD // 2, rows)), whole((HD // 2, rows)),
            whole((window, HD)), whole((window, HD)),
        ],
        out_specs=[
            pl.BlockSpec((rows, HD), lambda h: (0, h)), whole((window, HD)), whole((window, HD)),
        ],
        out_shape=[
            jax.ShapeDtypeStruct((rows, heads * HD), jnp.bfloat16),
            jax.ShapeDtypeStruct((window, HD), jnp.float32),
            jax.ShapeDtypeStruct((window, HD), jnp.float32),
        ],
        scratch_shapes=[pltpu.VMEM((rows // TILE, TILE + BACK, TILE), jnp.float32)],
        compiler_params=pltpu.CompilerParams(vmem_limit_bytes=40 * 1024 * 1024),
        cost_estimate=pl.CostEstimate(
            flops=work * HD * 10, bytes_accessed=4 * rows * heads * HD, transcendentals=work
        ),
    )(queries, grads, keys, values, keys_t, norm, delta, start, cosine, sine, dk_in, dv_in)


def undo_rotary(grad, cosine, sine):
    half = grad.shape[1] // 2
    first = grad[:, :half]
    second = grad[:, half:]
    return jnp.concatenate([first * cosine + second * sine, second * cosine - first * sine], axis=1)


def window_parts(row_count):
    parts = []
    shift = 1
    left = BACK
    while left > 0:
        count = min(left, row_count)
        parts.append((shift, row_count - count, count))
        left -= count
        shift += 1
    return parts


def swap_heads(array):
    return lax.all_to_all(array, "head", split_axis=1, concat_axis=0, tiled=True)


def on_device(
    layer_input, rot_queries, rot_keys, value_rows, attn_output, output_grad, log_norm, lengths
):
    head_count = log_norm.shape[1]
    head_devices = lax.axis_size("head")
    blocks = lax.axis_size("blk")
    local_count = rot_queries.shape[0]
    row_count = local_count * head_devices
    own_delta = jnp.sum(
        (output_grad.astype(jnp.float32) * attn_output.astype(jnp.float32)).reshape(
            local_count, HQ, HD
        ),
        axis=2,
    )
    high = lax.reduce_precision(own_delta, 8, 7)
    middle = lax.reduce_precision(own_delta - high, 8, 7)
    low = own_delta - high - middle
    by_head = lambda array: array.astype(jnp.bfloat16).reshape(local_count, head_devices, -1)
    packed = jnp.concatenate(
        [
            by_head(rot_keys), by_head(value_rows), by_head(high), by_head(middle), by_head(low),
            jnp.zeros((local_count, head_devices, HD - 3 * head_count), jnp.bfloat16),
        ],
        axis=2,
    ).reshape(local_count, -1)
    packed = swap_heads(packed)
    pairs = packed[:, : 2 * HD]
    terms = packed[:, 2 * HD :].astype(jnp.float32)
    delta = (
        terms[:, :head_count]
        + terms[:, head_count : 2 * head_count]
        + terms[:, 2 * head_count : 3 * head_count]
    )
    parts = window_parts(row_count)
    pieces = [pairs]
    for shift, first, count in parts:
        part = pairs[first : first + count]
        if shift < blocks:
            part = lax.ppermute(part, "blk", [(b, b + shift) for b in range(blocks - shift)])
        else:
            part = jnp.zeros_like(part)
        pieces.insert(0, part)
    queries = swap_heads(rot_queries)
    grads_out = swap_heads(output_grad)
    inputs = lax.all_to_all(layer_input, ("blk", "dp"), split_axis=1, concat_axis=0, tiled=True)
    groups = lax.axis_size("blk") * lax.axis_size("dp")
    inputs = lax.all_gather(inputs.reshape(groups, local_count, -1), "head", axis=1, tiled=True)
    inputs = inputs.reshape(groups * row_count, -1)
    keys_values = jnp.concatenate(pieces, axis=0)
    keys = keys_values[:, :HD]
    values = keys_values[:, HD:]

    lengths_row = lengths[0]
    ends = jnp.cumsum(lengths_row)
    first_row = lax.axis_index("blk") * row_count
    first, position = doc_place(
        ends, lengths_row, first_row + jnp.arange(row_count, dtype=jnp.int32)
    )
    start = (first - first_row + BACK)[None, :]
    steps_j = jnp.arange(HD // 2).astype(jnp.float32)
    inverse = jnp.exp(-math.log(500000.0) * 2.0 * steps_j / HD)
    angle = position.astype(jnp.float32)[:, None] * inverse[None, :]
    cosine = jnp.cos(angle) * SCALE
    sine = jnp.sin(angle) * SCALE

    zero = jnp.zeros((keys.shape[0], HD), jnp.float32)
    shared = (
        queries, grads_out, keys, values, keys.T, (log_norm.T * LOG2E)[:, None, :],
        delta.T[:, None, :], start, cosine.T, sine.T,
    )
    half = head_count // 2
    dq_first, dk_part, dv_part = attention(0, half, 704, *shared, zero, zero)
    all_first = lax.all_gather(dq_first, ("blk", "dp"), axis=0, tiled=True)
    dq_second, dk_part, dv_part = attention(half, half, 704, *shared, dk_part, dv_part)
    all_second = lax.all_gather(dq_second, ("blk", "dp"), axis=0, tiled=True)

    key_sums = jnp.concatenate([dk_part, dv_part], axis=1)
    total = key_sums[BACK:]
    at = BACK
    for shift, first, count in parts:
        at -= count
        if shift < blocks:
            got = lax.ppermute(
                key_sums[at : at + count].astype(jnp.bfloat16),
                "blk",
                [(b + shift, b) for b in range(blocks - shift)],
            ).astype(jnp.float32)
            total = total + jnp.pad(got, ((first, 0), (0, 0)))
    key_grads = jnp.concatenate(
        [undo_rotary(total[:, :HD], cosine, sine), total[:, HD:]], axis=1
    ).astype(jnp.bfloat16)
    all_keys = lax.all_gather(key_grads, ("blk", "dp"), axis=0, tiled=True)

    dw_first = contract_rows(inputs, all_first)
    dw_second = contract_rows(inputs, all_second)
    dw_keys = contract_rows(inputs, all_keys)
    return (
        jnp.concatenate([dw_first, dw_second], axis=1),
        dw_keys[:, :HD],
        dw_keys[:, HD:],
    )


def solution(mesh):
    placed = (
        P(("dp", "blk", "head"), None),
        P(("dp", "blk", "head"), None),
        P(("dp", "blk", "head"), None),
        P(("dp", "blk", "head"), None),
        P(("dp", "blk", "head"), None),
        P(("dp", "blk", "head"), None),
        P(("dp", "blk"), "head"),
        P("dp", None),
    )
    return jax.shard_map(
        on_device,
        mesh=mesh,
        in_specs=placed,
        out_specs=(P(("blk", "dp"), "head"), P(("blk", "dp"), "head"), P(("blk", "dp"), "head")),
        check_vma=False,
    )
```

time: 439 us -> 290 us (0.66)
  waiting for transfers between devices: 279 us -> 158 us
  matrix products: 54.6 us -> 15.7 us
  Pallas kernels: 0 us -> 19.3 us
  local copies, waits for them, and re-layouts: 25.4 us -> 20.4 us
    reduce_scatter x3 -> x0, waiting for transfers between devices: 259 us -> none  [the longest x1 208 us: on_device(): lax.psum_scatter(contract_rows(inputs_here, token_grads), ('blk', 'dp'),...]
    all_gather x1 -> x4, waiting for transfers between devices: 0.42 us -> 103 us  [the longest x1 42.5 us: on_device(): all_second = lax.all_gather(dq_second, ('blk', 'dp'), axis=0, tiled=True)]
    all_to_all x0 -> x1, blocking collectives: none -> 33 us  [on_device(): lax.all_to_all(layer_input, ('blk', 'dp'), split_axis=1, concat_axis=0, t...]
    all_gather x2 -> x0, blocking collectives: 31.7 us -> none  [the longest x1 16.8 us: on_device(): value_piece = lax.all_gather(values_here, 'blk', axis=0, tiled=True)]
    dot_general x24 -> x0, matrix products: 24.8 us -> none  [the longest x16 17.7 us: contract_cols(): lax.dot_general(left, right, (((1,), (1,)), ((), ())), preferred_element_...]
    pallas_call x0 -> x2, Pallas kernels: none -> 19.3 us  [attention(): pl.pallas_call(functools.partial(attention_kernel, chunk), grid=(heads,),...]
    ppermute x0 -> x6, waiting for transfers between devices: none -> 17.9 us  [the longest x3 17.9 us: on_device(): lax.ppermute(key_sums[at:at + count].astype(jnp.bfloat16), 'blk', [(b + s...]
    all_to_all x5 -> x3, waiting for transfers between devices: 19 us -> 36 us  [swap_heads(): lax.all_to_all(array, 'head', split_axis=1, concat_axis=0, tiled=True)]
  transfers between devices with their start and end apart: 9 -> 13, of which waited for: 8 -> 8; matrix products, arithmetic and copies ran while one was open for 3% -> 11% of each run, Pallas kernels for 0% -> 7%
where the time goes in v1:
time: 290 us; the launch traced here: 289 us
  waiting for transfers between devices  158 us (54%)
  blocking collectives  33 us (11%)
  starting transfers between devices  21.9 us (8%)
  local copies, waits for them, and re-layouts  20.4 us (7%)
  Pallas kernels  19.3 us (7%)
  matrix products  15.7 us (5%)
  between operations  14.1 us (5%)
  other arithmetic  6.71 us (2%)
    all_gather x1, waiting for transfers between devices, on_device(): all_second = lax.all_gather(dq_second, ('blk', 'dp'), axis=0, tiled=True)  42.5 us
    all_gather x1, waiting for transfers between devices, on_device(): all_first = lax.all_gather(dq_first, ('blk', 'dp'), axis=0, tiled=True)  42.1 us
    all_to_all x3, waiting for transfers between devices, swap_heads(): lax.all_to_all(array, 'head', split_axis=1, concat_axis=0, tiled=True)  36 us
    all_to_all x1, blocking collectives, on_device(): lax.all_to_all(layer_input, ('blk', 'dp'), split_axis=1, concat_axis=0, t...  33 us
    pallas_call x2, Pallas kernels, attention(): pl.pallas_call(functools.partial(attention_kernel, chunk), grid=(heads,),...  19.3 us
    all_gather x1, waiting for transfers between devices, on_device(): all_keys = lax.all_gather(key_grads, ('blk', 'dp'), axis=0, tiled=True)  18.6 us
    ppermute x3, waiting for transfers between devices, on_device(): lax.ppermute(key_sums[at:at + count].astype(jnp.bfloat16), 'blk', [(b + s...  17.9 us
    dot_general x3, matrix products, contract_rows(): lax.dot_general(left, right, (((0,), (0,)), ((), ())), preferred_element_...  15.7 us
  transfers between devices with their start and end apart: 13, of which 8 were waited for; matrix products, arithmetic and copies ran while one was open for 11% of the time, Pallas kernels for 7%

profile of v1, /device:TPU:0, one launch (start us, length us, event | category | flops | bytes accessed | tf_op | source)
XLA Modules:
  0.0 289.3 jit_solution(5996867806697222251)
XLA Ops:
  7.2 1.6 copy.90
  8.9 33.0 %all_to_all.70 = bf16[128,8,512]{0,2,1:T(8,128)(2,1)} all-to-all(bf16[128,8,512]{0,2,1:T(8,128)(2,1)S(1)} %bitcast.74), channel_id=1, replica_groups=mesh['head'=4,'blk'=4,'dp'=2] {'blk','dp'}, dimensions={1} | all-to-all | bytes 2097152 | tf_op jit(solution)/shard_map/all_to_all | solution.py:186
  47.4 3.7 %all-to-all-start.2 = ((bf16[128,4,384]{0,2,1:T(8,128)(2,1)}), bf16[128,4,384]{0,2,1:T(8,128)(2,1)S(1)}, u32[]{:S(2)}, u32[]{:S(2)}) async-start(bf16[128,4,384]{0,2,1:T(8,128)(2,1)} %broadcast_dynamic-update-slice_fusion), calls=%async_computation.2 | async-start | bytes 786432 | tf_op jit(solution)/shard_map/all_to_all | solution.py:139
  53.7 9.0 %all-to-all-done.2 = bf16[128,4,384]{0,2,1:T(8,128)(2,1)S(1)} async-done(((bf16[128,4,384]{0,2,1:T(8,128)(2,1)}), bf16[128,4,384]{0,2,1:T(8,128)(2,1)S(1)}, u32[]{:S(2)}, u32[]{:S(2)}) %all-to-all-start.2) | async-done | bytes 393248 | tf_op jit(solution)/shard_map/all_to_all | solution.py:139
  62.7 3.5 %all-to-all-start = ((bf16[128,4,1024]{2,0,1:T(8,128)(2,1)}), bf16[128,4,1024]{2,0,1:T(8,128)(2,1)S(1)}, u32[]{:S(2)}, u32[]{:S(2)}) async-start(bf16[128,4,1024]{2,0,1:T(8,128)(2,1)} %bitcast.62), calls=%async_computation | async-start | bytes 2097152 | tf_op jit(solution)/shard_map/all_to_all | solution.py:139
  67.5 1.3 collective-permute-start.1
  68.8 4.4 %collective-permute-start.2 = (bf16[512,256]{0,1:T(8,128)(2,1)S(1)}, bf16[512,256]{0,1:T(8,128)(2,1)S(1)}, u32[]{:S(2)}, u32[]{:S(2)}) collective-permute-start(bf16[512,256]{0,1:T(8,128)(2,1)S(1)} %slice.77), channel_id=1, source_target_pairs={{0,2},{2,4},{4,6},{1,3},{3,5},{5,7},{8,10},{10,12},{12,14},{9,11},... | collective-permute-start | bytes 786440 | tf_op jit(solution)/shard_map/ppermute | solution.py:180
  73.3 1.3 collective-permute-start
  74.6 4.1 %all-to-all-done = bf16[128,4,1024]{2,0,1:T(8,128)(2,1)S(1)} async-done(((bf16[128,4,1024]{2,0,1:T(8,128)(2,1)}), bf16[128,4,1024]{2,0,1:T(8,128)(2,1)S(1)}, u32[]{:S(2)}, u32[]{:S(2)}) %all-to-all-start) | async-done | bytes 1048608 | tf_op jit(solution)/shard_map/all_to_all | solution.py:139
  78.7 3.5 %all-to-all-start.1 = ((bf16[128,4,1024]{2,0,1:T(8,128)(2,1)}), bf16[128,4,1024]{2,0,1:T(8,128)(2,1)S(1)}, u32[]{:S(2)}, u32[]{:S(2)}) async-start(bf16[128,4,1024]{2,0,1:T(8,128)(2,1)} %bitcast.61), calls=%async_computation.1 | async-start | bytes 2097152 | tf_op jit(solution)/shard_map/all_to_all | solution.py:139
  83.5 1.3 copy.89.v_ref
  84.8 22.9 %all-to-all-done.1 = bf16[128,4,1024]{2,0,1:T(8,128)(2,1)S(1)} async-done(((bf16[128,4,1024]{2,0,1:T(8,128)(2,1)}), bf16[128,4,1024]{2,0,1:T(8,128)(2,1)S(1)}, u32[]{:S(2)}, u32[]{:S(2)}) %all-to-all-start.1) | async-done | bytes 1048608 | tf_op jit(solution)/shard_map/all_to_all | solution.py:139
  108.7 9.6 %shard_map.103 = (bf16[512,512]{1,0:T(8,128)(2,1)}, f32[1664,128]{1,0:T(8,128)S(1)}, f32[1664,128]{1,0:T(8,128)S(1)}) custom-call(bf16[512,1024]{1,0:T(8,128)(2,1)S(1)} %bitcast.63, bf16[512,1024]{1,0:T(8,128)(2,1)S(1)} %bitcast.65, bf16[1664,128]{1,0:T(8,128)(2,1)S(1)} %copy.88.k_ref, bf16[1664,128]{1,0:T(8,128)(2,1)S(1)} %copy.89.v_ref, ...), custom_call_target="tpu_custom_call" | custom-call | flops 3690987520 | bytes 1048576 | tf_op jit(solution)/shard_map/pallas_call | solution.py:95
  118.3 9.7 %shard_map.104 = (bf16[512,512]{1,0:T(8,128)(2,1)}, f32[1664,128]{1,0:T(8,128)S(1)}, f32[1664,128]{1,0:T(8,128)S(1)}) custom-call(bf16[512,1024]{1,0:T(8,128)(2,1)S(1)} %bitcast.64, bf16[512,1024]{1,0:T(8,128)(2,1)S(1)} %bitcast.66, bf16[1664,128]{1,0:T(8,128)(2,1)S(1)} %copy.88.k_ref, bf16[1664,128]{1,0:T(8,128)(2,1)S(1)} %copy.89.v_ref, ...), custom_call_target="tpu_custom_call" | custom-call | flops 3690987520 | bytes 1048576 | tf_op jit(solution)/shard_map/pallas_call | solution.py:95
  132.2 13.1 %collective-permute-done.5 = bf16[128,256]{1,0:T(8,128)(2,1)S(1)} collective-permute-done((bf16[128,256]{1,0:T(8,128)(2,1)S(1)}, bf16[128,256]{1,0:T(8,128)(2,1)S(1)}, u32[]{:S(2)}, u32[]{:S(2)}) %collective-permute-start.5) | collective-permute-done | bytes 65568 | tf_op jit(solution)/shard_map/ppermute | solution.py:224
  145.2 4.8 %collective-permute-done.4 = bf16[512,256]{1,0:T(8,128)(2,1)S(1)} collective-permute-done((bf16[512,256]{1,0:T(8,128)(2,1)S(1)}, bf16[512,256]{1,0:T(8,128)(2,1)S(1)}, u32[]{:S(2)}, u32[]{:S(2)}) %collective-permute-start.4) | collective-permute-done | bytes 262176 | tf_op jit(solution)/shard_map/ppermute | solution.py:224
  153.6 6.5 %copy.91 = bf16[8,512,512]{2,1,0:T(8,128)(2,1)} copy(bf16[8,512,512]{1,2,0:T(8,128)(2,1)} %all-gather.7.cloned.1.call-done) | data formatting | bytes 8388608 | tf_op jit(solution)/shard_map/all_gather | solution.py:188
  160.1 18.6 %all-gather.11.cloned.1.call-done = bf16[4096,256]{1,0:T(8,128)(2,1)} async-done(((bf16[512,256]{1,0:T(8,128)(2,1)}), bf16[4096,256]{1,0:T(8,128)(2,1)}) %all-gather.11.cloned.1.call-update) | async-done | bytes 2097168 | tf_op jit(solution)/shard_map/all_gather | solution.py:233
  178.8 4.1 %convolution_bitcast_fusion.2 = f32[512,256]{0,1:T(8,128)S(1)} fusion(bf16[4096,256]{1,0:T(8,128)(2,1)} %all-gather.11.cloned.1.call-done, bf16[4096,512]{1,0:T(8,128)(2,1)} %bitcast.69), kind=kOutput, calls=%fused_computation.4 | convolution fusion | flops 1073741824 | bytes 6815744 | tf_op jit(solution)/shard_map/dot_general | solution.py:23
  184.6 42.5 %all-gather.9.cloned.1.call-done = bf16[4096,512]{1,0:T(8,128)(2,1)} async-done(((bf16[512,512]{1,0:T(8,128)(2,1)}), bf16[4096,512]{1,0:T(8,128)(2,1)}) %all-gather.9.cloned.1.call-update) | async-done | bytes 4194320 | tf_op jit(solution)/shard_map/all_gather | solution.py:216
  227.0 5.8 %convolution_bitcast_fusion = f32[512,512]{0,1:T(8,128)S(1)} fusion(bf16[4096,512]{1,0:T(8,128)(2,1)} %all-gather.9.cloned.1.call-done, bf16[4096,512]{1,0:T(8,128)(2,1)} %bitcast.70), kind=kOutput, calls=%fused_computation.2 | convolution fusion | flops 2147483648 | bytes 9437184 | tf_op jit(solution)/shard_map/dot_general | solution.py:23
  232.9 42.1 %all-gather.5.cloned.1.call-done = bf16[4096,512]{1,0:T(8,128)(2,1)} async-done(((bf16[512,512]{1,0:T(8,128)(2,1)}), bf16[4096,512]{1,0:T(8,128)(2,1)}) %all-gather.5.cloned.1.call-update) | async-done | bytes 4194320 | tf_op jit(solution)/shard_map/all_gather | solution.py:214
  275.0 5.8 %convolution_bitcast_fusion.1 = f32[512,512]{0,1:T(8,128)S(1)} fusion(bf16[4096,512]{1,0:T(8,128)(2,1)} %all-gather.5.cloned.1.call-done, bf16[4096,512]{1,0:T(8,128)(2,1)} %bitcast.71), kind=kOutput, calls=%fused_computation.3 | convolution fusion | flops 2147483648 | bytes 9437184 | tf_op jit(solution)/shard_map/dot_general | solution.py:23
  281.0 1.8 copy.95
  (77 shorter events, 21.1 us)
Async XLA Ops:
  7.2 146.4 %all-gather.7.cloned.1.call-start = ((), (), s32[]{:S(2)}) async-start(), calls=%async_computation.5 | async-start | bytes 5242880 | tf_op jit(solution)/shard_map/all_gather | solution.py:188
  8.8 33.0 %copy-start.1 = (bf16[128,4096]{1,0:T(8,128)(2,1)S(1)}, bf16[128,4096]{1,0:T(8,128)(2,1)}, u32[]{:S(2)}) copy-start(bf16[128,4096]{1,0:T(8,128)(2,1)} %param.13) | copy-start | bytes 3145732
  8.8 33.0 %copy-start.3 = (bf16[128,4096]{1,0:T(8,128)(2,1)S(1)}, bf16[128,4096]{1,0:T(8,128)(2,1)}, u32[]{:S(2)}) copy-start(bf16[128,4096]{1,0:T(8,128)(2,1)} %param.12) | copy-start | bytes 3145732
  42.5 0.9 copy-start.4
  42.5 1.0 copy-start.5
  43.1 8.0 %copy-start.2 = (bf16[128,4096]{1,0:T(8,128)(2,1)S(1)}, bf16[128,4096]{1,0:T(8,128)(2,1)}, u32[]{:S(2)}) copy-start(bf16[128,4096]{1,0:T(8,128)(2,1)} %param.9) | copy-start | bytes 3145732
  47.4 15.3 %all-to-all-start.2 = ((bf16[128,4,384]{0,2,1:T(8,128)(2,1)}), bf16[128,4,384]{0,2,1:T(8,128)(2,1)S(1)}, u32[]{:S(2)}, u32[]{:S(2)}) async-start(bf16[128,4,384]{0,2,1:T(8,128)(2,1)} %broadcast_dynamic-update-slice_fusion), calls=%async_computation.2 | async-start | bytes 786432 | tf_op jit(solution)/shard_map/all_to_all | solution.py:139
  51.2 2.2 copy-start.6
  51.2 2.2 copy-start.7
  62.7 16.0 %all-to-all-start = ((bf16[128,4,1024]{2,0,1:T(8,128)(2,1)}), bf16[128,4,1024]{2,0,1:T(8,128)(2,1)S(1)}, u32[]{:S(2)}, u32[]{:S(2)}) async-start(bf16[128,4,1024]{2,0,1:T(8,128)(2,1)} %bitcast.62), calls=%async_computation | async-start | bytes 2097152 | tf_op jit(solution)/shard_map/all_to_all | solution.py:139
  67.5 14.8 %collective-permute-start.1 = (bf16[512,256]{0,1:T(8,128)(2,1)S(1)}, bf16[512,256]{0,1:T(8,128)(2,1)S(1)}, u32[]{:S(2)}, u32[]{:S(2)}) collective-permute-start(bf16[512,256]{0,1:T(8,128)(2,1)S(1)} %slice.77), channel_id=1, source_target_pairs={{0,4},{2,6},{1,5},{3,7},{8,12},{10,14},{9,13},{11,15},{16,20},{18,... | collective-permute-start | bytes 786440 | tf_op jit(solution)/shard_map/ppermute | solution.py:180
  68.8 13.5 %collective-permute-start.2 = (bf16[512,256]{0,1:T(8,128)(2,1)S(1)}, bf16[512,256]{0,1:T(8,128)(2,1)S(1)}, u32[]{:S(2)}, u32[]{:S(2)}) collective-permute-start(bf16[512,256]{0,1:T(8,128)(2,1)S(1)} %slice.77), channel_id=1, source_target_pairs={{0,2},{2,4},{4,6},{1,3},{3,5},{5,7},{8,10},{10,12},{12,14},{9,11},... | collective-permute-start | bytes 786440 | tf_op jit(solution)/shard_map/ppermute | solution.py:180
  73.3 9.0 %collective-permute-start = (bf16[128,256]{0,1:T(8,128)(2,1)S(1)}, bf16[128,256]{0,1:T(8,128)(2,1)S(1)}, u32[]{:S(2)}, u32[]{:S(2)}) collective-permute-start(bf16[128,256]{0,1:T(8,128)(2,1)S(1)} %slice.76), channel_id=1, source_target_pairs={{0,6},{1,7},{8,14},{9,15},{16,22},{17,23},{24,30},{25,31}} | collective-permute-start | bytes 196616 | tf_op jit(solution)/shard_map/ppermute | solution.py:180
  78.7 29.0 %all-to-all-start.1 = ((bf16[128,4,1024]{2,0,1:T(8,128)(2,1)}), bf16[128,4,1024]{2,0,1:T(8,128)(2,1)S(1)}, u32[]{:S(2)}, u32[]{:S(2)}) async-start(bf16[128,4,1024]{2,0,1:T(8,128)(2,1)} %bitcast.61), calls=%async_computation.1 | async-start | bytes 2097152 | tf_op jit(solution)/shard_map/all_to_all | solution.py:139
  82.2 96.6 %all-gather.11.cloned.1.call-start = ((), (), s32[]{:S(2)}) async-start(), calls=%async_computation.7 | async-start | bytes 2359296 | tf_op jit(solution)/shard_map/all_gather | solution.py:233
  107.8 0.9 copy-start
  128.2 17.0 %collective-permute-start.3 = (bf16[512,256]{1,0:T(8,128)(2,1)S(1)}, bf16[512,256]{1,0:T(8,128)(2,1)S(1)}, u32[]{:S(2)}, u32[]{:S(2)}) collective-permute-start(bf16[512,256]{1,0:T(8,128)(2,1)S(1)} %get-tuple-element.33), channel_id=1, source_target_pairs={{2,0},{4,2},{6,4},{3,1},{5,3},{7,5},{10,8},{12,10},{14,12},{11,9},... | collective-permute-start | bytes 786440 | tf_op jit(solution)/shard_map/ppermute | solution.py:224
  129.5 20.5 %collective-permute-start.4 = (bf16[512,256]{1,0:T(8,128)(2,1)S(1)}, bf16[512,256]{1,0:T(8,128)(2,1)S(1)}, u32[]{:S(2)}, u32[]{:S(2)}) collective-permute-start(bf16[512,256]{1,0:T(8,128)(2,1)S(1)} %get-tuple-element.34), channel_id=1, source_target_pairs={{4,0},{6,2},{5,1},{7,3},{12,8},{14,10},{13,9},{15,11},{20,16},{22,... | collective-permute-start | bytes 786440 | tf_op jit(solution)/shard_map/ppermute | solution.py:224
  130.9 14.4 %collective-permute-start.5 = (bf16[128,256]{1,0:T(8,128)(2,1)S(1)}, bf16[128,256]{1,0:T(8,128)(2,1)S(1)}, u32[]{:S(2)}, u32[]{:S(2)}) collective-permute-start(bf16[128,256]{1,0:T(8,128)(2,1)S(1)} %slice.87), channel_id=1, source_target_pairs={{6,0},{7,1},{14,8},{15,9},{22,16},{23,17},{30,24},{31,25}} | collective-permute-start | bytes 196616 | tf_op jit(solution)/shard_map/ppermute | solution.py:224
  152.3 74.8 %all-gather.9.cloned.1.call-start = ((), (), s32[]{:S(2)}) async-start(), calls=%async_computation.6 | async-start | bytes 4718592 | tf_op jit(solution)/shard_map/all_gather | solution.py:216
  153.0 122.0 %all-gather.5.cloned.1.call-start = ((), (), s32[]{:S(2)}) async-start(), calls=%async_computation.4 | async-start | bytes 4718592 | tf_op jit(solution)/shard_map/all_gather | solution.py:214
Sparse Core Ops, SparseCore 0:
  42.0 71.8 all-gather.6
  152.4 26.3 all-gather.10
  180.4 46.6 all-gather.8
  229.1 45.8 all-gather.4

commit v2 on v1

--- a/solution.py
+++ b/solution.py
@@ -116,6 +116,191 @@
     )(queries, grads, keys, values, keys_t, norm, delta, start, cosine, sine, dk_in, dv_in)
 
 
+MESH = pl.DeviceIdType.MESH
+
+
+def greet(peers):
+    barrier = pltpu.get_barrier_semaphore()
+    for peer in peers:
+        pl.semaphore_signal(barrier, inc=1, device_id=peer, device_id_type=MESH)
+    pl.semaphore_wait(barrier, len(peers))
+
+
+def ring_peers(axis, size):
+    here = lax.axis_index(axis)
+    return [{axis: lax.rem(here + step, size)} for step in range(1, size)]
+
+
+def group_peers(blocks, pairs):
+    block = lax.axis_index("blk")
+    side = lax.axis_index("dp")
+    peers = []
+    for step in range(1, blocks * pairs):
+        peers.append(
+            {
+                "blk": lax.rem(block + step // pairs, blocks),
+                "dp": lax.rem(side + step % pairs, pairs),
+            }
+        )
+    return peers
+
+
+def exchange_kernel(
+    sizes, parts, q_ref, g_ref, k_ref, v_ref, d_ref, x_ref,
+    qo_ref, go_ref, ko_ref, vo_ref, do_ref, xo_ref,
+    head_send, head_recv, own_sem, shift_send, shift_recv, group_send, group_recv,
+):
+    head_devices, blocks, pairs = sizes
+    me = lax.axis_index("head")
+    block = lax.axis_index("blk")
+    side = lax.axis_index("dp")
+    count = q_ref.shape[0]
+    head_list = ring_peers("head", head_devices)
+    group_list = group_peers(blocks, pairs)
+    greet(head_list + group_list)
+
+    def source(index, owner):
+        if index == 0:
+            return k_ref.at[:, pl.ds(pl.multiple_of(owner * HD, HD), HD)]
+        if index == 1:
+            return v_ref.at[:, pl.ds(pl.multiple_of(owner * HD, HD), HD)]
+        if index == 2:
+            rows = d_ref.shape[0] // head_devices
+            return d_ref.at[pl.ds(pl.multiple_of(owner * rows, 8), rows), :]
+        wide = q_ref.shape[1] // head_devices
+        columns = pl.ds(pl.multiple_of(owner * wide, HD), wide)
+        return (q_ref if index == 3 else g_ref).at[:, columns]
+
+    def target(index):
+        if index <= 1:
+            rows = pl.ds(pl.multiple_of(BACK + me * count, UNIT), count)
+            return (ko_ref if index == 0 else vo_ref).at[rows, :]
+        if index == 2:
+            return do_ref.at[:, pl.ds(pl.multiple_of(me * count, UNIT), count)]
+        rows = pl.ds(pl.multiple_of(me * count, UNIT), count)
+        return (qo_ref if index == 3 else go_ref).at[rows, :]
+
+    def head_copy(index, step):
+        owner = lax.rem(me + step, head_devices)
+        return pltpu.make_async_remote_copy(
+            src_ref=source(index, owner), dst_ref=target(index),
+            send_sem=head_send.at[index, step - 1], recv_sem=head_recv.at[index, step - 1],
+            device_id={"head": owner}, device_id_type=MESH,
+        )
+
+    def own_copy(index):
+        return pltpu.make_async_copy(source(index, me), target(index), own_sem.at[index])
+
+    wide = xo_ref.shape[2]
+    own_group = block * pairs + side
+
+    def group_copy(step):
+        peer = group_list[step - 1]
+        at = peer["blk"] * pairs + peer["dp"]
+        return pltpu.make_async_remote_copy(
+            src_ref=x_ref.at[:, pl.ds(pl.multiple_of(at * wide, HD), wide)],
+            dst_ref=xo_ref.at[own_group],
+            send_sem=group_send.at[step - 1], recv_sem=group_recv.at[step - 1],
+            device_id=peer, device_id_type=MESH,
+        )
+
+    own_x = pltpu.make_async_copy(
+        x_ref.at[:, pl.ds(pl.multiple_of(own_group * wide, HD), wide)],
+        xo_ref.at[own_group], own_sem.at[5],
+    )
+    head_steps = range(1, head_devices)
+    group_steps = range(1, blocks * pairs)
+    for index in (0, 1, 2):
+        own_copy(index).start()
+        for step in head_steps:
+            head_copy(index, step).start()
+    for index in (3, 4):
+        for step in head_steps:
+            head_copy(index, step).start()
+        own_copy(index).start()
+    for index in (0, 1):
+        own_copy(index).wait()
+        for step in head_steps:
+            head_copy(index, step).wait()
+
+    def shift_copy(which, number):
+        shift, first, rows = parts[number]
+        at = sum(part[2] for part in parts[number + 1 :])
+        ref = (ko_ref, vo_ref)[which]
+        return pltpu.make_async_remote_copy(
+            src_ref=ref.at[pl.ds(BACK + first, rows), :], dst_ref=ref.at[pl.ds(at, rows), :],
+            send_sem=shift_send.at[which, number], recv_sem=shift_recv.at[which, number],
+            device_id={"blk": block + shift}, device_id_type=MESH,
+        )
+
+    for number, (shift, first, rows) in enumerate(parts):
+        at = sum(part[2] for part in parts[number + 1 :])
+
+        @pl.when(block + shift < blocks)
+        def _():
+            for which in range(2):
+                shift_copy(which, number).start()
+
+        @pl.when(block < shift)
+        def _():
+            for ref in (ko_ref, vo_ref):
+                ref[pl.ds(at, rows), :] = jnp.zeros((rows, HD), jnp.bfloat16)
+
+    own_x.start()
+    for step in group_steps:
+        group_copy(step).start()
+    for index in (2, 3, 4):
+        own_copy(index).wait()
+        for step in head_steps:
+            head_copy(index, step).wait()
+    for number, (shift, first, rows) in enumerate(parts):
+
+        @pl.when(block + shift < blocks)
+        def _():
+            for which in range(2):
+                shift_copy(which, number).wait_send()
+
+        @pl.when(block >= shift)
+        def _():
+            for which in range(2):
+                shift_copy(which, number).wait_recv()
+
+    own_x.wait()
+    for step in group_steps:
+        group_copy(step).wait()
+
+
+def exchange(sizes, parts, queries, grads, keys, values, delta, inputs):
+    head_devices, blocks, pairs = sizes
+    count = queries.shape[0]
+    rows = count * head_devices
+    groups = blocks * pairs
+    anywhere = pl.BlockSpec(memory_space=pl.ANY)
+    inside = pl.BlockSpec(memory_space=pltpu.VMEM)
+    dma = pltpu.SemaphoreType.DMA
+    wide = queries.shape[1] // head_devices
+    return pl.pallas_call(
+        functools.partial(exchange_kernel, sizes, parts),
+        in_specs=[anywhere, anywhere, inside, inside, inside, anywhere],
+        out_specs=[anywhere, anywhere, inside, inside, inside, anywhere],
+        out_shape=[
+            jax.ShapeDtypeStruct((rows, wide), jnp.bfloat16),
+            jax.ShapeDtypeStruct((rows, wide), jnp.bfloat16),
+            jax.ShapeDtypeStruct((BACK + rows, HD), jnp.bfloat16),
+            jax.ShapeDtypeStruct((BACK + rows, HD), jnp.bfloat16),
+            jax.ShapeDtypeStruct((delta.shape[0] // head_devices, rows), jnp.float32),
+            jax.ShapeDtypeStruct((groups, count, inputs.shape[1] // groups), jnp.bfloat16),
+        ],
+        scratch_shapes=[
+            dma((5, head_devices - 1)), dma((5, head_devices - 1)), dma((6,)),
+            dma((2, len(parts))), dma((2, len(parts))), dma((groups - 1,)), dma((groups - 1,)),
+        ],
+        compiler_params=pltpu.CompilerParams(
+            collective_id=0, has_side_effects=True, vmem_limit_bytes=32 * 1024 * 1024
+        ),
+    )(queries, grads, keys, values, delta, inputs)
+
+
 def undo_rotary(grad, cosine, sine):
     half = grad.shape[1] // 2
     first = grad[:, :half]
@@ -153,43 +338,41 @@
         ),
         axis=2,
     )
-    high = lax.reduce_precision(own_delta, 8, 7)
-    middle = lax.reduce_precision(own_delta - high, 8, 7)
-    low = own_delta - high - middle
-    by_head = lambda array: array.astype(jnp.bfloat16).reshape(local_count, head_devices, -1)
-    packed = jnp.concatenate(
-        [
-            by_head(rot_keys), by_head(value_rows), by_head(high), by_head(middle), by_head(low),
-            jnp.zeros((local_count, head_devices, HD - 3 * head_count), jnp.bfloat16),
-        ],
-        axis=2,
-    ).reshape(local_count, -1)
-    packed = swap_heads(packed)
-    pairs = packed[:, : 2 * HD]
-    terms = packed[:, 2 * HD :].astype(jnp.float32)
-    delta = (
-        terms[:, :head_count]
-        + terms[:, head_count : 2 * head_count]
-        + terms[:, 2 * head_count : 3 * head_count]
-    )
     parts = window_parts(row_count)
-    pieces = [pairs]
-    for shift, first, count in parts:
-        part = pairs[first : first + count]
-        if shift < blocks:
-            part = lax.ppermute(part, "blk", [(b, b + shift) for b in range(blocks - shift)])
-        else:
-            part = jnp.zeros_like(part)
-        pieces.insert(0, part)
-    queries = swap_heads(rot_queries)
-    grads_out = swap_heads(output_grad)
-    inputs = lax.all_to_all(layer_input, ("blk", "dp"), split_axis=1, concat_axis=0, tiled=True)
-    groups = lax.axis_size("blk") * lax.axis_size("dp")
-    inputs = lax.all_gather(inputs.reshape(groups, local_count, -1), "head", axis=1, tiled=True)
-    inputs = inputs.reshape(groups * row_count, -1)
-    keys_values = jnp.concatenate(pieces, axis=0)
-    keys = keys_values[:, :HD]
-    values = keys_values[:, HD:]
+    pairs = lax.axis_size("dp")
+    groups = blocks * pairs
+    by_kernel = layer_input.shape[1] % (groups * HD) == 0 and pairs == 2
+    if by_kernel:
+        queries, grads_out, keys, values, delta, inputs = exchange(
+            (head_devices, blocks, pairs), parts, rot_queries, output_grad, rot_keys, value_rows,
+            own_delta.T, layer_input,
+        )
+    else:
+        queries = swap_heads(rot_queries)
+        grads_out = swap_heads(output_grad)
+        delta = swap_heads(own_delta).T
+        both = swap_heads(
+            jnp.concatenate(
+                [
+                    rot_keys.reshape(local_count, head_devices, -1),
+                    value_rows.reshape(local_count, head_devices, -1),
+                ],
+                axis=2,
+            ).reshape(local_count, -1)
+        )
+        pieces = [both]
+        for shift, first, count in parts:
+            part = both[first : first + count]
+            if shift < blocks:
+                part = lax.ppermute(part, "blk", [(b, b + shift) for b in range(blocks - shift)])
+            else:
+                part = jnp.zeros_like(part)
+            pieces.insert(0, part)
+        keys_values = jnp.concatenate(pieces, axis=0)
+        keys = keys_values[:, :HD]
+        values = keys_values[:, HD:]
+        inputs = lax.all_to_all(layer_input, ("blk", "dp"), split_axis=1, concat_axis=0, tiled=True)
+        inputs = inputs.reshape(groups, local_count, -1)
 
     lengths_row = lengths[0]
     ends = jnp.cumsum(lengths_row)
@@ -207,7 +390,7 @@
     zero = jnp.zeros((keys.shape[0], HD), jnp.float32)
     shared = (
         queries, grads_out, keys, values, keys.T, (log_norm.T * LOG2E)[:, None, :],
-        delta.T[:, None, :], start, cosine.T, sine.T,
+        delta[:, None, :], start, cosine.T, sine.T,
     )
     half = head_count // 2
     dq_first, dk_part, dv_part = attention(0, half, 704, *shared, zero, zero)
@@ -215,6 +398,7 @@
     dq_second, dk_part, dv_part = attention(half, half, 704, *shared, dk_part, dv_part)
     all_second = lax.all_gather(dq_second, ("blk", "dp"), axis=0, tiled=True)
 
+    inputs = lax.all_gather(inputs, "head", axis=1, tiled=True).reshape(groups * row_count, -1)
     key_sums = jnp.concatenate([dk_part, dv_part], axis=1)
     total = key_sums[BACK:]
     at = BACK

time: 290 us -> 307 us (1.059)
  Pallas kernels: 19.3 us -> 60.1 us
  waiting for transfers between devices: 158 us -> 195 us
  blocking collectives: 33 us -> 0 us
  starting transfers between devices: 21.9 us -> 4.21 us
  local copies, waits for them, and re-layouts: 20.4 us -> 10.8 us
    all_gather x1, waiting for transfers between devices: 0.02 us -> 54.1 us  [on_device(): lax.all_gather(inputs, 'head', axis=1, tiled=True)]
    pallas_call x0 -> x1, Pallas kernels: none -> 40.6 us  [exchange(): pl.pallas_call(functools.partial(exchange_kernel, sizes, parts), in_specs...]
    all_to_all x3 -> x0, waiting for transfers between devices: 36 us -> none  [swap_heads(): lax.all_to_all(array, 'head', split_axis=1, concat_axis=0, tiled=True)]
    all_to_all x1 -> x0, blocking collectives: 33 us -> none  [on_device(): lax.all_to_all(layer_input, ('blk', 'dp'), split_axis=1, concat_axis=0, t...]
    all_to_all x3 -> x0, starting transfers between devices: 10.8 us -> none  [swap_heads(): lax.all_to_all(array, 'head', split_axis=1, concat_axis=0, tiled=True)]
    ppermute x3, waiting for transfers between devices: 17.9 us -> 28.3 us  [on_device(): lax.ppermute(key_sums[at:at + count].astype(jnp.bfloat16), 'blk', [(b + s...]
    ppermute x3 -> x0, starting transfers between devices: 6.96 us -> none  [on_device(): lax.ppermute(part, 'blk', [(b, b + shift) for b in range(blocks - shift)])]
    all_gather x1 -> x0, local copies, waits for them, and re-layouts: 6.51 us -> none  [on_device(): lax.all_gather(inputs.reshape(groups, local_count, -1), 'head', axis=1, t...]
  transfers between devices with their start and end apart: 13 -> 7, of which waited for: 8 -> 6; matrix products, arithmetic and copies ran while one was open for 11% -> 4% of each run, Pallas kernels for 7% -> 0%
where the time goes in v2:
time: 307 us
  waiting for transfers between devices  195 us (64%)
  Pallas kernels  60.1 us (20%)
  matrix products  15.8 us (5%)
  between operations  14.1 us (5%)
  local copies, waits for them, and re-layouts  10.8 us (4%)
  other arithmetic  7.42 us (2%)
  starting transfers between devices  4.21 us (1%)
    all_gather x1, waiting for transfers between devices, on_device(): lax.all_gather(inputs, 'head', axis=1, tiled=True)  54.1 us
    all_gather x1, waiting for transfers between devices, on_device(): all_second = lax.all_gather(dq_second, ('blk', 'dp'), axis=0, tiled=True)  43.8 us
    all_gather x1, waiting for transfers between devices, on_device(): all_first = lax.all_gather(dq_first, ('blk', 'dp'), axis=0, tiled=True)  42.1 us
    pallas_call x1, Pallas kernels, exchange(): pl.pallas_call(functools.partial(exchange_kernel, sizes, parts), in_specs...  40.6 us
    ppermute x3, waiting for transfers between devices, on_device(): lax.ppermute(key_sums[at:at + count].astype(jnp.bfloat16), 'blk', [(b + s...  28.3 us
    all_gather x1, waiting for transfers between devices, on_device(): all_keys = lax.all_gather(key_grads, ('blk', 'dp'), axis=0, tiled=True)  24.7 us
    pallas_call x2, Pallas kernels, attention(): pl.pallas_call(functools.partial(attention_kernel, chunk), grid=(heads,),...  19.5 us
    dot_general x3, matrix products, contract_rows(): lax.dot_general(left, right, (((0,), (0,)), ((), ())), preferred_element_...  15.8 us
  transfers between devices with their start and end apart: 7, of which 6 were waited for; matrix products, arithmetic and copies ran while one was open for 4% of the time, Pallas kernels for 0%

profile of v2, /device:TPU:0, one launch (start us, length us, event | category | flops | bytes accessed | tf_op | source)
XLA Modules:
  0.0 307.1 jit_solution(296141387146680982)
XLA Ops:
  7.2 1.8 multiply_bitcast_fusion
  9.1 1.7 copy.23
  10.7 2.4 reduce_sum.18
  13.2 40.6 %shard_map.103 = (bf16[512,1024]{1,0:T(8,128)(2,1)S(1)}, bf16[512,1024]{1,0:T(8,128)(2,1)S(1)}, bf16[1664,128]{1,0:T(8,128)(2,1)S(1)}, bf16[1664,128]{1,0:T(8,12...) custom-call(bf16[128,4096]{1,0:T(8,128)(2,1)S(1)} %copy-done.1, bf16[128,4096]{1,0:T(8,128)(2,1)S(1)} %copy-done, ...), custom_call_target="tpu_custom_call" | custom-call | tf_op jit(solution)/shard_map/pallas_call | solution.py:282
  54.6 1.0 copy-done.7
  55.6 1.0 copy-done.9
  57.4 1.4 copy.20
  59.8 1.2 copy-done.10
  61.0 9.7 %shard_map.104 = (bf16[512,512]{1,0:T(8,128)(2,1)}, f32[1664,128]{1,0:T(8,128)S(1)}, f32[1664,128]{1,0:T(8,128)S(1)}) custom-call(bf16[512,1024]{1,0:T(8,128)(2,1)S(1)} %copy-done.8, bf16[512,1024]{1,0:T(8,128)(2,1)S(1)} %copy-done.10, bf16[1664,128]{1,0:T(8,128)(2,1)S(1)} %copy-done.4, bf16[1664,128]{1,0:T(8,128)(2,1)S(1)} %copy-done.13, ...), custom_call_target="tpu_custom_call" | custom-call | flops 3690987520 | bytes 1048576 | tf_op jit(solution)/shard_map/pallas_call | solution.py:95
  70.7 9.7 %shard_map.105 = (bf16[512,512]{1,0:T(8,128)(2,1)}, f32[1664,128]{1,0:T(8,128)S(1)}, f32[1664,128]{1,0:T(8,128)S(1)}) custom-call(bf16[512,1024]{1,0:T(8,128)(2,1)S(1)} %copy-done.8, bf16[512,1024]{1,0:T(8,128)(2,1)S(1)} %copy-done.11, bf16[1664,128]{1,0:T(8,128)(2,1)S(1)} %copy-done.4, bf16[1664,128]{1,0:T(8,128)(2,1)S(1)} %copy-done.13, ...), custom_call_target="tpu_custom_call" | custom-call | flops 3690987520 | bytes 1048576 | tf_op jit(solution)/shard_map/pallas_call | solution.py:95
  80.7 1.3 collective-permute-start
  82.0 1.3 collective-permute-start.1
  83.3 1.3 collective-permute-start.2
  84.6 24.4 %collective-permute-done.2 = bf16[128,256]{1,0:T(8,128)(2,1)S(1)} collective-permute-done((bf16[128,256]{1,0:T(8,128)(2,1)S(1)}, bf16[128,256]{1,0:T(8,128)(2,1)S(1)}, u32[]{:S(2)}, u32[]{:S(2)}) %collective-permute-start.2) | collective-permute-done | bytes 65568 | tf_op jit(solution)/shard_map/ppermute | solution.py:408
  109.1 3.8 %collective-permute-done.1 = bf16[512,256]{1,0:T(8,128)(2,1)S(1)} collective-permute-done((bf16[512,256]{1,0:T(8,128)(2,1)S(1)}, bf16[512,256]{1,0:T(8,128)(2,1)S(1)}, u32[]{:S(2)}, u32[]{:S(2)}) %collective-permute-start.1) | collective-permute-done | bytes 262176 | tf_op jit(solution)/shard_map/ppermute | solution.py:408
  113.0 1.2 fusion.6
  117.2 24.7 %all-gather.11.cloned.1.call-done = bf16[4096,256]{1,0:T(8,128)(2,1)} async-done(((bf16[512,256]{1,0:T(8,128)(2,1)}), bf16[4096,256]{1,0:T(8,128)(2,1)}) %all-gather.11.cloned.1.call-update) | async-done | bytes 2097168 | tf_op jit(solution)/shard_map/all_gather | solution.py:417
  142.0 54.1 %all-gather.5.cloned.1.call-done = bf16[8,512,512]{2,1,0:T(8,128)(2,1)} async-done(((bf16[8,128,512]{2,1,0:T(8,128)(2,1)}), bf16[8,512,512]{2,1,0:T(8,128)(2,1)}) %all-gather.5.cloned.1.call-update) | async-done | bytes 4194320 | tf_op jit(solution)/shard_map/all_gather | solution.py:401
  196.0 4.2 %fusion.18 = f32[512,256]{1,0:T(8,128)S(1)} fusion(bf16[4096,512]{1,0:T(8,128)(2,1)} %bitcast.27, bf16[4096,256]{1,0:T(8,128)(2,1)} %all-gather.11.cloned.1.call-done), kind=kOutput, calls=%fused_computation.35 | convolution fusion | flops 1073741824 | bytes 6815744 | tf_op jit(solution)/shard_map/dot_general | solution.py:23
  201.0 43.8 %all-gather.9.cloned.1.call-done = bf16[4096,512]{1,0:T(8,128)(2,1)} async-done(((bf16[512,512]{1,0:T(8,128)(2,1)}), bf16[4096,512]{1,0:T(8,128)(2,1)}) %all-gather.9.cloned.1.call-update) | async-done | bytes 4194320 | tf_op jit(solution)/shard_map/all_gather | solution.py:399
  244.8 5.8 %fusion.17 = f32[512,512]{0,1:T(8,128)S(1)} fusion(bf16[4096,512]{1,0:T(8,128)(2,1)} %bitcast.28, bf16[4096,512]{1,0:T(8,128)(2,1)} %all-gather.9.cloned.1.call-done), kind=kOutput, calls=%fused_computation.34 | convolution fusion | flops 2147483648 | bytes 9437184 | tf_op jit(solution)/shard_map/dot_general | solution.py:23
  250.7 42.1 %all-gather.7.cloned.1.call-done = bf16[4096,512]{1,0:T(8,128)(2,1)} async-done(((bf16[512,512]{1,0:T(8,128)(2,1)}), bf16[4096,512]{1,0:T(8,128)(2,1)}) %all-gather.7.cloned.1.call-update) | async-done | bytes 4194320 | tf_op jit(solution)/shard_map/all_gather | solution.py:397
  292.7 5.8 %fusion.16 = f32[512,512]{0,1:T(8,128)S(1)} fusion(bf16[4096,512]{1,0:T(8,128)(2,1)} %bitcast.29, bf16[4096,512]{1,0:T(8,128)(2,1)} %all-gather.7.cloned.1.call-done), kind=kOutput, calls=%fused_computation.33 | convolution fusion | flops 2147483648 | bytes 9437184 | tf_op jit(solution)/shard_map/dot_general | solution.py:23
  298.8 1.8 copy.22
  (59 shorter events, 6.8 us)
Async XLA Ops:
  7.2 134.8 %all-gather.11.cloned.1.call-start = ((), (), s32[]{:S(2)}) async-start(), calls=%async_computation.3 | async-start | bytes 2359296 | tf_op jit(solution)/shard_map/all_gather | solution.py:417
  9.0 4.1 %copy-start.2 = (bf16[128,4096]{1,0:T(8,128)(2,1)S(1)}, bf16[128,4096]{1,0:T(8,128)(2,1)}, u32[]{:S(2)}) copy-start(bf16[128,4096]{1,0:T(8,128)(2,1)} %x_ref.1) | copy-start | bytes 3145732
  9.0 4.1 %copy-start.6 = (bf16[128,512]{1,0:T(8,128)(2,1)S(1)}, bf16[128,512]{1,0:T(8,128)(2,1)}, u32[]{:S(2)}) copy-start(bf16[128,512]{1,0:T(8,128)(2,1)} %v_ref.1) | copy-start | bytes 393220
  10.7 2.4 copy-start
  10.7 2.5 copy-start.1
  10.7 2.5 copy-start.5
  13.2 45.6 %copy-start.15 = (s32[1,3]{1,0:T(1,128)S(1)}, s32[1,3]{1,0:T(1,128)}, u32[]{:S(2)}) copy-start(s32[1,3]{1,0:T(1,128)} %param.15) | copy-start | bytes 40
  13.2 45.8 %copy-start.14 = (f32[512,8]{0,1:T(8,128)S(1)}, f32[512,8]{0,1:T(8,128)}, u32[]{:S(2)}) copy-start(f32[512,8]{0,1:T(8,128)} %param.14) | copy-start | bytes 49156
  53.9 0.7 copy-start.3
  54.6 1.0 copy-start.7
  55.6 1.0 copy-start.9
  56.6 0.8 copy-start.12
  57.4 2.4 copy-start.4
  57.4 2.4 copy-start.8
  57.4 2.4 copy-start.13
  59.8 1.2 copy-start.10
  61.0 9.7 %copy-start.11 = (bf16[512,1024]{1,0:T(8,128)(2,1)S(1)}, bf16[512,1024]{1,0:T(8,128)(2,1)}, u32[]{:S(2)}) copy-start(bf16[512,1024]{1,0:T(8,128)(2,1)} %copy-done.9) | copy-start | bytes 3145732
  80.7 28.3 %collective-permute-start = (bf16[512,256]{1,0:T(8,128)(2,1)S(1)}, bf16[512,256]{1,0:T(8,128)(2,1)S(1)}, u32[]{:S(2)}, u32[]{:S(2)}) collective-permute-start(bf16[512,256]{1,0:T(8,128)(2,1)S(1)} %get-tuple-element.39), channel_id=1, source_target_pairs={{2,0},{4,2},{6,4},{3,1},{5,3},{7,5},{10,8},{12,10},{14,12},{11,9},... | collective-permute-start | bytes 786440 | tf_op jit(solution)/shard_map/ppermute | solution.py:408
  82.0 30.9 %collective-permute-start.1 = (bf16[512,256]{1,0:T(8,128)(2,1)S(1)}, bf16[512,256]{1,0:T(8,128)(2,1)S(1)}, u32[]{:S(2)}, u32[]{:S(2)}) collective-permute-start(bf16[512,256]{1,0:T(8,128)(2,1)S(1)} %get-tuple-element.40), channel_id=1, source_target_pairs={{4,0},{6,2},{5,1},{7,3},{12,8},{14,10},{13,9},{15,11},{20,16},{22,... | collective-permute-start | bytes 786440 | tf_op jit(solution)/shard_map/ppermute | solution.py:408
  83.3 25.7 %collective-permute-start.2 = (bf16[128,256]{1,0:T(8,128)(2,1)S(1)}, bf16[128,256]{1,0:T(8,128)(2,1)S(1)}, u32[]{:S(2)}, u32[]{:S(2)}) collective-permute-start(bf16[128,256]{1,0:T(8,128)(2,1)S(1)} %slice.46), channel_id=1, source_target_pairs={{6,0},{7,1},{14,8},{15,9},{22,16},{23,17},{30,24},{31,25}} | collective-permute-start | bytes 196616 | tf_op jit(solution)/shard_map/ppermute | solution.py:408
  115.1 80.9 %all-gather.5.cloned.1.call-start = ((), (), s32[]{:S(2)}) async-start(), calls=%async_computation | async-start | bytes 5242880 | tf_op jit(solution)/shard_map/all_gather | solution.py:401
  115.9 128.9 %all-gather.9.cloned.1.call-start = ((), (), s32[]{:S(2)}) async-start(), calls=%async_computation.2 | async-start | bytes 4718592 | tf_op jit(solution)/shard_map/all_gather | solution.py:399
  116.6 176.1 %all-gather.7.cloned.1.call-start = ((), (), s32[]{:S(2)}) async-start(), calls=%async_computation.1 | async-start | bytes 4718592 | tf_op jit(solution)/shard_map/all_gather | solution.py:397
Sparse Core Ops, SparseCore 0:
  115.3 26.6 all-gather.10
  143.8 52.1 all-gather.4
  197.6 47.1 all-gather.8
  246.8 45.8 all-gather.6

commit v3 on v2

--- a/solution.py
+++ b/solution.py
@@ -301,6 +301,224 @@
     )(queries, grads, keys, values, delta, inputs)
 
 
+def gather_kernel(
+    sizes, parts, dq_ref, kp_ref, ko_ref, cos_ref, sin_ref, x_ref,
+    dwq_ref, dwk_ref, dwv_ref,
+    land, got, inputs, turned, total, keys_sum,
+    key_send, key_recv, x_send, x_recv, own_sem, up_send, up_recv, down_send, down_recv,
+    side_send, side_recv,
+):
+    head_devices, blocks, pairs = sizes
+    me = lax.axis_index("head")
+    block = lax.axis_index("blk")
+    side = lax.axis_index("dp")
+    other = 1 - side
+    rows = dq_ref.shape[0]
+    count = rows // head_devices
+    wide = 2 * HD
+    chunks = land.shape[1]
+    head_list = ring_peers("head", head_devices)
+    greet(head_list + ring_peers("blk", blocks) + [{"dp": other}])
+
+    def key_copy(number):
+        shift, first, size = parts[number]
+        at = sum(part[2] for part in parts[number + 1 :])
+        return pltpu.make_async_remote_copy(
+            src_ref=kp_ref.at[pl.ds(at, size), :], dst_ref=got.at[pl.ds(at, size), :],
+            send_sem=key_send.at[number], recv_sem=key_recv.at[number],
+            device_id={"blk": block - shift}, device_id_type=MESH,
+        )
+
+    def chain_copy(hop, owner, chunk, up):
+        spot = land.at[owner * pairs + side, chunk]
+        return pltpu.make_async_remote_copy(
+            src_ref=spot, dst_ref=spot,
+            send_sem=(up_send if up else down_send).at[hop, chunk],
+            recv_sem=(up_recv if up else down_recv).at[hop, chunk],
+            device_id={"blk": block + 1 if up else block - 1}, device_id_type=MESH,
+        )
+
+    def side_copy(owner, chunk, from_side):
+        spot = land.at[owner * pairs + from_side, chunk]
+        return pltpu.make_async_remote_copy(
+            src_ref=spot, dst_ref=spot, send_sem=side_send.at[owner, chunk],
+            recv_sem=side_recv.at[owner, chunk], device_id={"dp": other}, device_id_type=MESH,
+        )
+
+    def x_copy(step):
+        mine = pl.ds(pl.multiple_of(me * count, UNIT), count)
+        return pltpu.make_async_remote_copy(
+            src_ref=x_ref, dst_ref=inputs.at[:, mine, :], send_sem=x_send.at[step - 1],
+            recv_sem=x_recv.at[step - 1], device_id=head_list[step - 1], device_id_type=MESH,
+        )
+
+    def push(owner, hop, chunk):
+        @pl.when((block + 1 < blocks) & (owner <= block))
+        def _():
+            chain_copy(hop, owner, chunk, True).start()
+
+        @pl.when((block >= 1) & (owner >= block))
+        def _():
+            chain_copy(hop, owner, chunk, False).start()
+
+        side_copy(owner, chunk, side).start()
+
+    for number, (shift, first, size) in enumerate(parts):
+        at = sum(part[2] for part in parts[number + 1 :])
+
+        @pl.when(block >= shift)
+        def _():
+            key_copy(number).start()
+
+        @pl.when(block + shift >= blocks)
+        def _():
+            got[pl.ds(at, size), :] = jnp.zeros((size, wide), jnp.bfloat16)
+
+    own_group = block * pairs + side
+    for chunk in range(chunks - 1):
+        land[own_group, chunk] = dq_ref[:, chunk * wide : (chunk + 1) * wide]
+        push(block, 0, chunk)
+    own_x = pltpu.make_async_copy(
+        x_ref, inputs.at[:, pl.ds(pl.multiple_of(me * count, UNIT), count), :], own_sem.at[0]
+    )
+    own_x.start()
+    for step in range(1, head_devices):
+        x_copy(step).start()
+    keys_sum[...] = ko_ref[...]
+    for number, (shift, first, size) in enumerate(parts):
+        at = sum(part[2] for part in parts[number + 1 :])
+
+        @pl.when(block + shift < blocks)
+        def _():
+            key_copy(number).wait_recv()
+
+        keys_sum[first : first + size, :] += got[pl.ds(at, size), :].astype(jnp.float32)
+
+    dk = keys_sum[:, :HD]
+    dk = dk * cos_ref[...] + pltpu.roll(dk, HD // 2, 1) * sin_ref[...]
+    land[own_group, chunks - 1, :, :HD] = dk.astype(jnp.bfloat16)
+    land[own_group, chunks - 1, :, HD:] = keys_sum[:, HD:].astype(jnp.bfloat16)
+    push(block, 0, chunks - 1)
+
+    own_x.wait()
+    for step in range(1, head_devices):
+        x_copy(step).wait_recv()
+    total[...] = jnp.zeros_like(total)
+
+    def multiply(group):
+        turned[...] = inputs[group].T
+
+        @pl.loop(0, chunks)
+        def _(chunk):
+            total[chunk] += jnp.dot(
+                turned[...], land[group, chunk], preferred_element_type=jnp.float32
+            )
+
+    def take(owner, hop, up):
+        @pl.loop(0, chunks)
+        def _(chunk):
+            chain_copy(hop, owner, chunk, up).wait_recv()
+
+            @pl.when((block + 1 < blocks) if up else (block >= 1))
+            def _():
+                chain_copy(hop + 1, owner, chunk, up).start()
+
+            side_copy(owner, chunk, side).start()
+
+    def finish(owner):
+        multiply(owner * pairs + side)
+
+        @pl.loop(0, chunks)
+        def _(chunk):
+            side_copy(owner, chunk, other).wait_recv()
+
+        multiply(owner * pairs + other)
+
+    finish(block)
+    for hop in range(blocks - 1):
+        below = block - 1 - hop
+        above = block + 1 + hop
+
+        @pl.when(below >= 0)
+        def _():
+            take(below, hop, True)
+
+        @pl.when(above < blocks)
+        def _():
+            take(above, hop, False)
+
+        @pl.when(below >= 0)
+        def _():
+            finish(below)
+
+        @pl.when(above < blocks)
+        def _():
+            finish(above)
+
+    for chunk in range(chunks - 1):
+        dwq_ref[:, chunk * wide : (chunk + 1) * wide] = total[chunk]
+    dwk_ref[...] = total[chunks - 1, :, :HD]
+    dwv_ref[...] = total[chunks - 1, :, HD:]
+
+    for number, (shift, first, size) in enumerate(parts):
+
+        @pl.when(block >= shift)
+        def _():
+            key_copy(number).wait_send()
+
+    for step in range(1, head_devices):
+        x_copy(step).wait_send()
+
+    @pl.loop(0, chunks)
+    def _(chunk):
+        for owner in range(blocks):
+            side_copy(owner, chunk, side).wait_send()
+        for hop in range(blocks - 1):
+
+            @pl.when((block + 1 < blocks) & (block >= hop))
+            def _():
+                chain_copy(hop, block - hop, chunk, True).wait_send()
+
+            @pl.when((block >= 1) & (block + hop < blocks))
+            def _():
+                chain_copy(hop, block + hop, chunk, False).wait_send()
+
+
+def gather_multiply(sizes, parts, dq, key_parts, own_keys, cosine, sine, inputs):
+    head_devices, blocks, pairs = sizes
+    rows = dq.shape[0]
+    groups, count, features = inputs.shape
+    chunks = dq.shape[1] // (2 * HD) + 1
+    inside = pl.BlockSpec(memory_space=pltpu.VMEM)
+    dma = pltpu.SemaphoreType.DMA
+    return pl.pallas_call(
+        functools.partial(gather_kernel, sizes, parts),
+        in_specs=[inside] * 6,
+        out_specs=[inside] * 3,
+        out_shape=[
+            jax.ShapeDtypeStruct((features, dq.shape[1]), jnp.float32),
+            jax.ShapeDtypeStruct((features, HD), jnp.float32),
+            jax.ShapeDtypeStruct((features, HD), jnp.float32),
+        ],
+        scratch_shapes=[
+            pltpu.VMEM((groups, chunks, rows, 2 * HD), jnp.bfloat16),
+            pltpu.VMEM(key_parts.shape, jnp.bfloat16),
+            pltpu.VMEM((groups, rows, features), jnp.bfloat16),
+            pltpu.VMEM((features, rows), jnp.bfloat16),
+            pltpu.VMEM((chunks, features, 2 * HD), jnp.float32),
+            pltpu.VMEM(own_keys.shape, jnp.float32),
+            dma((len(parts),)), dma((len(parts),)),
+            dma((head_devices - 1,)), dma((head_devices - 1,)), dma((1,)),
+            dma((blocks, chunks)), dma((blocks, chunks)),
+            dma((blocks, chunks)), dma((blocks, chunks)),
+            dma((blocks, chunks)), dma((blocks, chunks)),
+        ],
+        compiler_params=pltpu.CompilerParams(
+            collective_id=1, has_side_effects=True, vmem_limit_bytes=48 * 1024 * 1024
+        ),
+    )(dq, key_parts, own_keys, cosine, sine, inputs)
+
+
 def undo_rotary(grad, cosine, sine):
     half = grad.shape[1] // 2
     first = grad[:, :half]
@@ -392,6 +610,16 @@
         queries, grads_out, keys, values, keys.T, (log_norm.T * LOG2E)[:, None, :],
         delta[:, None, :], start, cosine.T, sine.T,
     )
+    if by_kernel:
+        dq, dk_part, dv_part = attention(0, head_count, 704, *shared, zero, zero)
+        key_sums = jnp.concatenate([dk_part, dv_part], axis=1)
+        return tuple(
+            gather_multiply(
+                (head_devices, blocks, pairs), parts, dq, key_sums[:BACK].astype(jnp.bfloat16),
+                key_sums[BACK:], jnp.concatenate([cosine, cosine], axis=1),
+                jnp.concatenate([sine, -sine], axis=1), inputs,
+            )
+        )
     half = head_count // 2
     dq_first, dk_part, dv_part = attention(0, half, 704, *shared, zero, zero)
     all_first = lax.all_gather(dq_first, ("blk", "dp"), axis=0, tiled=True)

time: 307 us -> 208 us (0.68)
  waiting for transfers between devices: 195 us -> 0 us
  Pallas kernels: 60.1 us -> 187 us
  matrix products: 15.8 us -> 0 us
  between operations: 14.1 us -> 0.88 us
  starting transfers between devices: 4.21 us -> 0 us
  local copies, waits for them, and re-layouts: 10.8 us -> 13.9 us
    all_gather x4 -> x0, waiting for transfers between devices: 165 us -> none  [the longest x1 54.1 us: on_device(): lax.all_gather(inputs, 'head', axis=1, tiled=True)]
    pallas_call x0 -> x1, Pallas kernels: none -> 129 us  [gather_multiply(): pl.pallas_call(functools.partial(gather_kernel, sizes, parts), in_specs=[...]
    ppermute x3 -> x0, waiting for transfers between devices: 28.3 us -> none  [on_device(): lax.ppermute(key_sums[at:at + count].astype(jnp.bfloat16), 'blk', [(b + s...]
    dot_general x3 -> x0, matrix products: 15.8 us -> none  [contract_rows(): lax.dot_general(left, right, (((0,), (0,)), ((), ())), preferred_element_...]
    unnamed x35, local copies, waits for them, and re-layouts: 8.31 us -> 12.3 us
    ppermute x3 -> x0, starting transfers between devices: 3.88 us -> none  [on_device(): lax.ppermute(key_sums[at:at + count].astype(jnp.bfloat16), 'blk', [(b + s...]
    pallas_call x2 -> x1, Pallas kernels: 19.5 us -> 17.6 us  [attention(): pl.pallas_call(functools.partial(attention_kernel, chunk), grid=(heads,),...]
  transfers between devices with their start and end apart: 7 -> 0, of which waited for: 6 -> 0; matrix products, arithmetic and copies ran while one was open for 4% -> 0% of each run, Pallas kernels for 0% -> 0%
where the time goes in v3:
time: 208 us
  Pallas kernels  187 us (90%)
  local copies, waits for them, and re-layouts  13.9 us (7%)
  other arithmetic  6.2 us (3%)
    pallas_call x1, Pallas kernels, gather_multiply(): pl.pallas_call(functools.partial(gather_kernel, sizes, parts), in_specs=[...  129 us
    pallas_call x1, Pallas kernels, exchange(): pl.pallas_call(functools.partial(exchange_kernel, sizes, parts), in_specs...  40.5 us
    pallas_call x1, Pallas kernels, attention(): pl.pallas_call(functools.partial(attention_kernel, chunk), grid=(heads,),...  17.6 us
    unnamed x35, local copies, waits for them, and re-layouts  12.3 us

profile of v3, /device:TPU:0, one launch (start us, length us, event | category | flops | bytes accessed | tf_op | source)
XLA Modules:
  0.0 207.8 jit_solution(13626064210360243063)
XLA Ops:
  0.6 1.8 multiply_bitcast_fusion
  2.4 1.7 copy.16
  4.1 2.4 %reduce_sum.18 = f32[128,32]{1,0:T(8,128)S(1)} reduce(f32[128,32,128]{2,1,0:T(8,128)} %bitcast.14, f32[]{:T(128)} %constant.9.clone.1), dimensions={2}, to_apply=%region_0.0 | reduce | flops 520192 | bytes 2113540 | tf_op jit(solution)/shard_map/reduce_sum | solution.py:553
  6.6 1.2 copy-done.2
  7.8 40.5 %shard_map.103 = (bf16[512,1024]{1,0:T(8,128)(2,1)S(1)}, bf16[512,1024]{1,0:T(8,128)(2,1)S(1)}, bf16[1664,128]{1,0:T(8,128)(2,1)S(1)}, bf16[1664,128]{1,0:T(8,12...) custom-call(bf16[128,4096]{1,0:T(8,128)(2,1)S(1)} %copy-done.1, bf16[128,4096]{1,0:T(8,128)(2,1)S(1)} %copy-done, ...), custom_call_target="tpu_custom_call" | custom-call | tf_op jit(solution)/shard_map/pallas_call | solution.py:282
  48.4 0.8 copy-done.3
  49.1 1.0 copy-done.7
  50.1 1.0 copy-done.9
  51.1 0.8 copy-done.11
  51.8 1.4 copy.15
  53.3 0.2 reduce-window.8
  53.4 0.1 select_reduce_fusion
  53.5 0.5 fusion.3
  54.3 1.2 copy-done.10
  55.5 17.6 %shard_map.104 = (bf16[512,1024]{1,0:T(8,128)(2,1)S(1)}, f32[1664,128]{1,0:T(8,128)S(1)}, f32[1664,128]{1,0:T(8,128)S(1)}) custom-call(bf16[512,1024]{1,0:T(8,128)(2,1)S(1)} %copy-done.8, bf16[512,1024]{1,0:T(8,128)(2,1)S(1)} %copy-done.10, bf16[1664,128]{1,0:T(8,128)(2,1)S(1)} %copy-done.4, bf16[1664,128]{1,0:T(8,128)(2,1)S(1)} %copy-done.12, ...), custom_call_target="tpu_custom_call" | custom-call | flops 7381975040 | bytes 2097152 | tf_op jit(solution)/shard_map/pallas_call | solution.py:95
  73.1 0.1 constant_dynamic-update-slice_fusion.1
  73.1 0.1 constant_dynamic-update-slice_fusion
  73.2 0.1 slice.12.kp_ref
  73.3 1.0 fusion.1
  74.3 0.2 pad_maximum_fusion
  74.5 128.7 %shard_map.105 = (f32[512,1024]{1,0:T(8,128)}, f32[512,128]{1,0:T(8,128)S(1)}, f32[512,128]{1,0:T(8,128)S(1)}) custom-call(bf16[512,1024]{1,0:T(8,128)(2,1)S(1)} %get-tuple-element.17.dq_ref, bf16[1152,256]{1,0:T(8,128)(2,1)S(1)} %slice.12.kp_ref, f32[512,256]{1,0:T(8,128)S(1)} %slice.10.ko_ref, f32[512,128]{1,0:T(8,128)S(1)} %get-tuple-element.28.cos_ref, ...), custom_call_target="tpu_custom_call" | custom-call | tf_op jit(solution)/shard_map/pallas_call | solution.py:494
  203.3 3.2 %copy.21 = f32[512,1024]{1,0:T(8,128)} copy(f32[512,1024]{1,0:T(8,128)} %get-tuple-element.33) | data formatting | bytes 4194304
  206.4 0.7 copy.22
  207.1 0.7 copy.23
  (33 shorter events, 0.2 us)
Async XLA Ops:
  2.4 4.1 %copy-start.6 = (bf16[128,512]{1,0:T(8,128)(2,1)S(1)}, bf16[128,512]{1,0:T(8,128)(2,1)}, u32[]{:S(2)}) copy-start(bf16[128,512]{1,0:T(8,128)(2,1)} %v_ref.1) | copy-start | bytes 393220
  4.1 2.4 %copy-start = (bf16[128,4096]{1,0:T(8,128)(2,1)S(1)}, bf16[128,4096]{1,0:T(8,128)(2,1)}, u32[]{:S(2)}) copy-start(bf16[128,4096]{1,0:T(8,128)(2,1)} %g_ref.1) | copy-start | bytes 3145732
  4.1 2.4 %copy-start.1 = (bf16[128,4096]{1,0:T(8,128)(2,1)S(1)}, bf16[128,4096]{1,0:T(8,128)(2,1)}, u32[]{:S(2)}) copy-start(bf16[128,4096]{1,0:T(8,128)(2,1)} %q_ref.1) | copy-start | bytes 3145732
  4.1 2.5 %copy-start.5 = (bf16[128,512]{1,0:T(8,128)(2,1)S(1)}, bf16[128,512]{1,0:T(8,128)(2,1)}, u32[]{:S(2)}) copy-start(bf16[128,512]{1,0:T(8,128)(2,1)} %k_ref.1) | copy-start | bytes 393220
  6.6 1.2 copy-start.2
  7.8 45.4 %copy-start.14 = (s32[1,3]{1,0:T(1,128)S(1)}, s32[1,3]{1,0:T(1,128)}, u32[]{:S(2)}) copy-start(s32[1,3]{1,0:T(1,128)} %param.15) | copy-start | bytes 40
  7.8 46.3 %copy-start.13 = (f32[512,8]{0,1:T(8,128)S(1)}, f32[512,8]{0,1:T(8,128)}, u32[]{:S(2)}) copy-start(f32[512,8]{0,1:T(8,128)} %param.14) | copy-start | bytes 49156
  48.4 0.8 copy-start.3
  49.1 1.0 copy-start.7
  50.1 1.0 copy-start.9
  51.1 0.8 copy-start.11
  51.8 2.4 %copy-start.4 = (bf16[1664,128]{1,0:T(8,128)(2,1)S(1)}, bf16[1664,128]{1,0:T(8,128)(2,1)}, u32[]{:S(2)}) copy-start(bf16[1664,128]{1,0:T(8,128)(2,1)} %copy-done.3) | copy-start | bytes 1277956
  51.8 2.4 %copy-start.8 = (bf16[512,1024]{1,0:T(8,128)(2,1)S(1)}, bf16[512,1024]{1,0:T(8,128)(2,1)}, u32[]{:S(2)}) copy-start(bf16[512,1024]{1,0:T(8,128)(2,1)} %copy-done.7) | copy-start | bytes 3145732
  51.8 2.4 %copy-start.12 = (bf16[1664,128]{1,0:T(8,128)(2,1)S(1)}, bf16[1664,128]{1,0:T(8,128)(2,1)}, u32[]{:S(2)}) copy-start(bf16[1664,128]{1,0:T(8,128)(2,1)} %copy-done.11) | copy-start | bytes 1277956
  54.2 1.2 copy-start.10

commit v4 on v3

--- a/solution.py
+++ b/solution.py
@@ -109,7 +109,7 @@
             jax.ShapeDtypeStruct((window, HD), jnp.float32),
         ],
         scratch_shapes=[pltpu.VMEM((rows // TILE, TILE + BACK, TILE), jnp.float32)],
-        compiler_params=pltpu.CompilerParams(vmem_limit_bytes=40 * 1024 * 1024),
+        compiler_params=pltpu.CompilerParams(vmem_limit_bytes=58 * 1024 * 1024),
         cost_estimate=pl.CostEstimate(
             flops=work * HD * 10, bytes_accessed=4 * rows * heads * HD, transcendentals=work
         ),
@@ -146,9 +146,9 @@
 
 
 def exchange_kernel(
-    sizes, parts, q_ref, g_ref, k_ref, v_ref, d_ref, x_ref,
+    sizes, parts, q_ref, g_ref, k_ref, v_ref, o_ref, x_ref,
     qo_ref, go_ref, ko_ref, vo_ref, do_ref, xo_ref,
-    head_send, head_recv, own_sem, shift_send, shift_recv, group_send, group_recv,
+    d_ref, head_send, head_recv, own_sem, shift_send, shift_recv, group_send, group_recv,
 ):
     head_devices, blocks, pairs = sizes
     me = lax.axis_index("head")
@@ -210,10 +210,13 @@
     )
     head_steps = range(1, head_devices)
     group_steps = range(1, blocks * pairs)
-    for index in (0, 1, 2):
+    for index in (0, 1):
         own_copy(index).start()
         for step in head_steps:
             head_copy(index, step).start()
+    own_x.start()
+    for step in group_steps:
+        group_copy(step).start()
     for index in (3, 4):
         for step in head_steps:
             head_copy(index, step).start()
@@ -246,9 +249,13 @@
             for ref in (ko_ref, vo_ref):
                 ref[pl.ds(at, rows), :] = jnp.zeros((rows, HD), jnp.bfloat16)
 
-    own_x.start()
-    for step in group_steps:
-        group_copy(step).start()
+    for head in range(d_ref.shape[0]):
+        columns = slice(head * HD, (head + 1) * HD)
+        product = g_ref[:, columns].astype(jnp.float32) * o_ref[:, columns].astype(jnp.float32)
+        d_ref[head : head + 1, :] = jnp.sum(product.T, axis=0, keepdims=True)
+    own_copy(2).start()
+    for step in head_steps:
+        head_copy(2, step).start()
     for index in (2, 3, 4):
         own_copy(index).wait()
         for step in head_steps:
@@ -270,7 +277,7 @@
         group_copy(step).wait()
 
 
-def exchange(sizes, parts, queries, grads, keys, values, delta, inputs):
+def exchange(sizes, parts, queries, grads, keys, values, outputs, inputs):
     head_devices, blocks, pairs = sizes
     count = queries.shape[0]
     rows = count * head_devices
@@ -281,24 +288,25 @@
     wide = queries.shape[1] // head_devices
     return pl.pallas_call(
         functools.partial(exchange_kernel, sizes, parts),
-        in_specs=[anywhere, anywhere, inside, inside, inside, anywhere],
+        in_specs=[anywhere, inside, inside, inside, inside, anywhere],
         out_specs=[anywhere, anywhere, inside, inside, inside, anywhere],
         out_shape=[
             jax.ShapeDtypeStruct((rows, wide), jnp.bfloat16),
             jax.ShapeDtypeStruct((rows, wide), jnp.bfloat16),
             jax.ShapeDtypeStruct((BACK + rows, HD), jnp.bfloat16),
             jax.ShapeDtypeStruct((BACK + rows, HD), jnp.bfloat16),
-            jax.ShapeDtypeStruct((delta.shape[0] // head_devices, rows), jnp.float32),
+            jax.ShapeDtypeStruct((HQ // head_devices, rows), jnp.float32),
             jax.ShapeDtypeStruct((groups, count, inputs.shape[1] // groups), jnp.bfloat16),
         ],
         scratch_shapes=[
+            pltpu.VMEM((HQ, count), jnp.float32),
             dma((5, head_devices - 1)), dma((5, head_devices - 1)), dma((6,)),
             dma((2, len(parts))), dma((2, len(parts))), dma((groups - 1,)), dma((groups - 1,)),
         ],
         compiler_params=pltpu.CompilerParams(
             collective_id=0, has_side_effects=True, vmem_limit_bytes=32 * 1024 * 1024
         ),
-    )(queries, grads, keys, values, delta, inputs)
+    )(queries, grads, keys, values, outputs, inputs)
 
 
 def gather_kernel(
@@ -550,12 +558,6 @@
     blocks = lax.axis_size("blk")
     local_count = rot_queries.shape[0]
     row_count = local_count * head_devices
-    own_delta = jnp.sum(
-        (output_grad.astype(jnp.float32) * attn_output.astype(jnp.float32)).reshape(
-            local_count, HQ, HD
-        ),
-        axis=2,
-    )
     parts = window_parts(row_count)
     pairs = lax.axis_size("dp")
     groups = blocks * pairs
@@ -563,11 +565,17 @@
     if by_kernel:
         queries, grads_out, keys, values, delta, inputs = exchange(
             (head_devices, blocks, pairs), parts, rot_queries, output_grad, rot_keys, value_rows,
-            own_delta.T, layer_input,
+            attn_output, layer_input,
         )
     else:
         queries = swap_heads(rot_queries)
         grads_out = swap_heads(output_grad)
+        own_delta = jnp.sum(
+            (output_grad.astype(jnp.float32) * attn_output.astype(jnp.float32)).reshape(
+                local_count, HQ, HD
+            ),
+            axis=2,
+        )
         delta = swap_heads(own_delta).T
         both = swap_heads(
             jnp.concatenate(

time: 208 us -> 207 us (level)
  local copies, waits for them, and re-layouts: 13.9 us -> 18.7 us
  Pallas kernels: 187 us -> 184 us
  other arithmetic: 6.2 us -> 3.32 us
    pallas_call x1, Pallas kernels: 40.5 us -> 35.8 us  [exchange(): pl.pallas_call(functools.partial(exchange_kernel, sizes, parts), in_specs...]
    unnamed x35 -> x32, local copies, waits for them, and re-layouts: 12.3 us -> 15.4 us
    reduce_sum x1 -> x0, other arithmetic: 2.35 us -> none  [on_device(): jnp.sum((output_grad.astype(jnp.float32) * attn_output.astype(jnp.float32...]
    pallas_call x1, Pallas kernels: 17.6 us -> 19.9 us  [attention(): pl.pallas_call(functools.partial(attention_kernel, chunk), grid=(heads,),...]
where the time goes in v4:
time: 207 us
  Pallas kernels  184 us (89%)
  local copies, waits for them, and re-layouts  18.7 us (9%)
  other arithmetic  3.32 us (2%)
    pallas_call x1, Pallas kernels, gather_multiply(): pl.pallas_call(functools.partial(gather_kernel, sizes, parts), in_specs=[...  128 us
    pallas_call x1, Pallas kernels, exchange(): pl.pallas_call(functools.partial(exchange_kernel, sizes, parts), in_specs...  35.8 us
    pallas_call x1, Pallas kernels, attention(): pl.pallas_call(functools.partial(attention_kernel, chunk), grid=(heads,),...  19.9 us
    unnamed x32, local copies, waits for them, and re-layouts  15.4 us

profile of v4, /device:TPU:0, one launch (start us, length us, event | category | flops | bytes accessed | tf_op | source)
XLA Modules:
  0.0 206.6 jit_solution(3332836257427959772)
XLA Ops:
  0.6 1.2 copy-done
  1.9 1.2 copy-done.1
  3.1 1.2 copy-done.2
  4.3 1.2 copy-done.3
  5.5 0.9 copy-done.6
  6.4 0.9 copy-done.7
  7.3 35.8 %shard_map.103 = (bf16[512,1024]{1,0:T(8,128)(2,1)S(1)}, bf16[512,1024]{1,0:T(8,128)(2,1)S(1)}, bf16[1664,128]{1,0:T(8,128)(2,1)S(1)}, bf16[1664,128]{1,0:T(8,12...) custom-call(bf16[128,4096]{1,0:T(8,128)(2,1)S(1)} %copy-done, bf16[128,4096]{1,0:T(8,128)(2,1)S(1)} %copy-done.1, ...), custom_call_target="tpu_custom_call" | custom-call | tf_op jit(solution)/shard_map/pallas_call | solution.py:289
  43.2 1.0 copy-done.8
  44.2 1.0 copy-done.9
  45.1 0.8 copy-done.10
  45.9 1.0 copy.12
  47.1 0.6 subtract_convert_fusion
  47.7 1.3 fusion.3
  49.0 0.6 broadcast_in_dim.7.delta_ref
  49.6 0.6 broadcast_in_dim.6.norm_ref
  50.2 1.0 broadcast_in_dim.16.dk_in_ref.dv_in_ref
  51.2 19.9 %shard_map.104 = (bf16[512,1024]{1,0:T(8,128)(2,1)}, f32[1664,128]{1,0:T(8,128)}, f32[1664,128]{1,0:T(8,128)}) custom-call(bf16[512,1024]{1,0:T(8,128)(2,1)} %copy-done.8, bf16[512,1024]{1,0:T(8,128)(2,1)} %copy-done.9, bf16[1664,128]{1,0:T(8,128)(2,1)} %copy-done.5, bf16[1664,128]{1,0:T(8,128)(2,1)} %copy-done.10, bf16[128,1664]{1,0:T(8,128)(2,1)} %bitcast.7, ...), custom_call_target="tpu_custom_call" | custom-call | flops 7381975040 | bytes 2097152 | tf_op jit(solution)/shard_map/pallas_call | solution.py:95
  71.1 1.3 constant_dynamic-update-slice_fusion.1
  72.7 1.0 fusion.1
  73.7 0.2 pad_maximum_fusion
  73.9 128.1 %shard_map.105 = (f32[512,1024]{1,0:T(8,128)}, f32[512,128]{1,0:T(8,128)S(1)}, f32[512,128]{1,0:T(8,128)S(1)}) custom-call(bf16[512,1024]{1,0:T(8,128)(2,1)S(1)} %copy-done.4, bf16[1152,256]{1,0:T(8,128)(2,1)S(1)} %slice.12.kp_ref, f32[512,256]{1,0:T(8,128)S(1)} %slice.10.ko_ref, f32[512,128]{1,0:T(8,128)S(1)} %get-tuple-element.28.cos_ref, ...), custom_call_target="tpu_custom_call" | custom-call | tf_op jit(solution)/shard_map/pallas_call | solution.py:502
  202.1 3.2 %copy.17 = f32[512,1024]{1,0:T(8,128)} copy(f32[512,1024]{1,0:T(8,128)} %get-tuple-element.33) | data formatting | bytes 4194304
  205.2 0.7 copy.18
  205.9 0.7 copy.19
  (27 shorter events, 0.6 us)
Async XLA Ops:
  0.6 1.2 copy-start
  1.9 1.2 copy-start.1
  3.1 1.2 copy-start.2
  4.3 1.2 copy-start.3
  5.5 0.9 copy-start.6
  6.4 0.9 copy-start.7
  7.3 39.5 %copy-start.13 = (s32[1,3]{1,0:T(1,128)S(1)}, s32[1,3]{1,0:T(1,128)}, u32[]{:S(2)}) copy-start(s32[1,3]{1,0:T(1,128)} %param.15) | copy-start | bytes 40
  7.3 42.2 %copy-start.12 = (f32[512,8]{0,1:T(8,128)S(1)}, f32[512,8]{0,1:T(8,128)}, u32[]{:S(2)}) copy-start(f32[512,8]{0,1:T(8,128)} %param.14) | copy-start | bytes 49156
  43.2 1.0 copy-start.8
  44.1 1.0 copy-start.9
  45.1 0.8 copy-start.10
  45.9 5.3 %copy-start.5 = (bf16[1664,128]{1,0:T(8,128)(2,1)}, bf16[1664,128]{1,0:T(8,128)(2,1)S(1)}, u32[]{:S(2)}) copy-start(bf16[1664,128]{1,0:T(8,128)(2,1)S(1)} %get-tuple-element.14.k_ref) | copy-start | bytes 1277956
  71.1 1.4 copy-start.11
  72.7 1.3 copy-start.4
